TPU v7x, 32 devices: a whole 2x2x4 slice. The times are simulated.
32 devices in a mesh: dp: 4 (over y, x), fsdp: 8 (over z, core).
Axes of the slice: x: 2, y: 2, z: 4, core: 2. Of those that a mesh axis runs over, the one named last changes fastest.
Arguments:
- tokens: bfloat16 [32768, 768], P(('dp', 'fsdp')), may hold values from -6 to 6
- lengths: int32 [64, 4], P(('dp', 'fsdp')), may hold values from 0 to 512, as said below
- bucket: int32 [32], replicated, may hold values from 0 to 1, as said below
- position_table: bfloat16 [512, 768], P(None, 'fsdp'), may hold values from -3 to 3
- in_projection: bfloat16 [768, 2304], P('fsdp'), may hold values from -0.21875 to 0.21875
- query_bias: bfloat16 [768], P('fsdp'), may hold values from -1.25 to 1.25
- value_bias: bfloat16 [768], P('fsdp'), may hold values from -1.25 to 1.25
- out_projection: bfloat16 [768, 768], P('fsdp'), may hold values from -0.875 to 0.875
- out_bias: bfloat16 [768], P('fsdp'), may hold values from -1.25 to 1.25
- first_gain: bfloat16 [768], P('fsdp'), may hold values from 0.5 to 1.5
- first_shift: bfloat16 [768], P('fsdp'), may hold values from -0.625 to 0.625
- up_projection: bfloat16 [768, 3072], P('fsdp'), may hold values from -0.21875 to 0.21875
- up_bias: bfloat16 [3072], P('fsdp'), may hold values from -1.25 to 1.25
- down_projection: bfloat16 [3072, 768], P('fsdp'), may hold values from -0.109375 to 0.109375
- down_bias: bfloat16 [768], P('fsdp'), may hold values from -1.25 to 1.25
- second_gain: bfloat16 [768], P('fsdp'), may hold values from 0.5 to 1.5
- second_shift: bfloat16 [768], P('fsdp'), may hold values from -0.625 to 0.625
Outputs:
- loss: float32 [], replicated
- pooled: float32 [256, 768], P(('dp', 'fsdp'))
- tokens_grad: float32 [32768, 768], P(('dp', 'fsdp'))
- position_table_grad: float32 [512, 768], P(None, 'fsdp')
- in_projection_grad: float32 [768, 2304], P('fsdp')
- query_bias_grad: float32 [768], P('fsdp')
- value_bias_grad: float32 [768], P('fsdp')
- out_projection_grad: float32 [768, 768], P('fsdp')
- out_bias_grad: float32 [768], P('fsdp')
- first_gain_grad: float32 [768], P('fsdp')
- first_shift_grad: float32 [768], P('fsdp')
- up_projection_grad: float32 [768, 3072], P('fsdp')
- up_bias_grad: float32 [3072], P('fsdp')
- down_projection_grad: float32 [3072, 768], P('fsdp')
- down_bias_grad: float32 [768], P('fsdp')
- second_gain_grad: float32 [768], P('fsdp')
- second_shift_grad: float32 [768], P('fsdp')
Inputs may be any that keep to these rules, and one draw needn't show every extreme that they name: bucket[p] = 1: groups 2p and 2p+1 each hold one sequence of up to 512 positions, the first a query, the second its passage; bucket[p] = 0: both hold four sequences of up to 128 positions, query and passage alternating. Both kinds occur in every draw. lengths[g, s] is the true length of the sequence that begins at slot s of group g: 32 to 128 in four-sequence groups; 128 to 512 in slot 0 of one-sequence groups, 0 in their other slots. A long sequence of 512 and a short one of 128 occur in every draw.
All inputs are finite; a program needn't handle non-finite values.
Results may differ from a plain program's by a relative error of at most 0.015.
Values may be sent and summed in bfloat16 or wider, within the bound.
A program may use at most 192 MiB of HBM per device.

v0:
```python
import jax
import jax.numpy as jnp
from jax import lax
from jax.sharding import PartitionSpec as P

H = 12


highest = lax.Precision.HIGHEST
narrow = jnp.bfloat16
single = jnp.float32


def norm_forward(value, gain, shift):
    mean = jnp.mean(value, -1, keepdims=True)
    centred = value - mean
    spread = jnp.mean(centred * centred, -1, keepdims=True)
    return centred * lax.rsqrt(spread + 1e-06) * gain + shift


def exact_gelu(value):
    return jax.nn.gelu(value, approximate=False)


def normalize_rows(pooled):
    return pooled * lax.rsqrt(jnp.sum(pooled * pooled, -1, keepdims=True) + 1e-06)


def group_state(block, long_flag, lengths_row, weights):
    (
        table,
        w_in,
        query_bias,
        value_bias,
        w_out,
        out_bias,
        gain_one,
        shift_one,
        w_up,
        up_bias,
        w_down,
        down_bias,
        gain_two,
        shift_two,
    ) = weights
    count, width = block.shape
    slot = count // 4
    head_size = width // H
    places = jnp.arange(count, dtype=jnp.int32)
    segment = jnp.where(long_flag > 0, 0, places // slot)
    inside = jnp.where(long_flag > 0, places, places % slot)
    choose = segment[:, None] == jnp.arange(4, dtype=jnp.int32)[None, :]
    live = inside < jnp.sum(jnp.where(choose, lengths_row[None, :], 0), 1)
    picker = jnp.transpose((choose & live[:, None]).astype(single))
    positions = jnp.where(long_flag > 0, table, jnp.tile(table[:slot], (4, 1)))
    resid = block.astype(single) + positions.astype(single)
    x_low = resid.astype(narrow)
    in_bias = jnp.concatenate([query_bias, jnp.zeros_like(query_bias), value_bias]).astype(single)
    mixed = (jnp.dot(x_low, w_in, preferred_element_type=single) + in_bias).astype(narrow)
    query = mixed[:, :width].reshape(count, H, head_size)
    keys = mixed[:, width : 2 * width].reshape(count, H, head_size)
    vals = mixed[:, 2 * width :].reshape(count, H, head_size)
    allowed = (segment[:, None] == segment[None, :]) & live[None, :]
    scores = jnp.einsum("qhd,khd->hqk", query, keys, preferred_element_type=single) * head_size ** (
        -0.5
    )
    scores = jnp.where(allowed[None], scores, -1000000000.0)
    top = jnp.max(scores, -1, keepdims=True)
    raised = jnp.exp(scores - top)
    prob = raised / jnp.sum(raised, -1, keepdims=True)
    prob_low = prob.astype(narrow)
    context = jnp.einsum("hqk,khd->qhd", prob_low, vals, preferred_element_type=single)
    context = context.reshape(count, width).astype(narrow)
    attended = jnp.dot(context, w_out, preferred_element_type=single) + out_bias.astype(single)
    first_in = resid + attended
    hidden = norm_forward(first_in, gain_one.astype(single), shift_one.astype(single))
    hidden_low = hidden.astype(narrow)
    upward = jnp.dot(hidden_low, w_up, preferred_element_type=single) + up_bias.astype(single)
    active = exact_gelu(upward).astype(narrow)
    downward = jnp.dot(active, w_down, preferred_element_type=single) + down_bias.astype(single)
    second_in = hidden + downward
    output = norm_forward(second_in, gain_two.astype(single), shift_two.astype(single))
    return {
        "picker": picker,
        "x_low": x_low,
        "query": query,
        "keys": keys,
        "vals": vals,
        "prob": prob,
        "prob_low": prob_low,
        "context": context,
        "first_in": first_in,
        "hidden_low": hidden_low,
        "upward": upward,
        "active": active,
        "second_in": second_in,
        "output": output,
    }


def group_pool(block, long_flag, lengths_row, weights):
    state = group_state(block, long_flag, lengths_row, weights)
    divisor = jnp.maximum(lengths_row, 1).astype(single)
    return jnp.dot(state["picker"], state["output"], precision=highest) / divisor[:, None]


def group_backward(block, long_flag, lengths_row, pooled_grad, weights):
    (
        table,
        w_in,
        query_bias,
        value_bias,
        w_out,
        out_bias,
        gain_one,
        shift_one,
        w_up,
        up_bias,
        w_down,
        down_bias,
        gain_two,
        shift_two,
    ) = weights
    state = group_state(block, long_flag, lengths_row, weights)
    count, width = block.shape
    slot = count // 4
    head_size = width // H
    scale = head_size ** (-0.5)
    divisor = jnp.maximum(lengths_row, 1).astype(single)
    output_grad = jnp.dot(
        jnp.transpose(state["picker"]), pooled_grad / divisor[:, None], precision=highest
    )
    _, second_back = jax.vjp(
        norm_forward, state["second_in"], gain_two.astype(single), shift_two.astype(single)
    )
    second_grad, gain_two_grad, shift_two_grad = second_back(output_grad)
    down_low = second_grad.astype(narrow)
    down_bias_grad = jnp.sum(down_low.astype(single), 0)
    down_grad = jnp.einsum("tf,td->fd", state["active"], down_low, preferred_element_type=single)
    active_grad = jnp.einsum("td,fd->tf", down_low, w_down, preferred_element_type=single)
    _, gelu_back = jax.vjp(exact_gelu, state["upward"])
    up_low = gelu_back(active_grad)[0].astype(narrow)
    up_bias_grad = jnp.sum(up_low.astype(single), 0)
    up_grad = jnp.einsum("td,tf->df", state["hidden_low"], up_low, preferred_element_type=single)
    hidden_grad = second_grad + jnp.einsum("tf,df->td", up_low, w_up, preferred_element_type=single)
    _, first_back = jax.vjp(
        norm_forward, state["first_in"], gain_one.astype(single), shift_one.astype(single)
    )
    first_grad, gain_one_grad, shift_one_grad = first_back(hidden_grad)
    attend_low = first_grad.astype(narrow)
    out_bias_grad = jnp.sum(attend_low.astype(single), 0)
    out_grad = jnp.einsum("te,td->ed", state["context"], attend_low, preferred_element_type=single)
    context_grad = jnp.einsum("td,ed->te", attend_low, w_out, preferred_element_type=single)
    context_grad = context_grad.astype(narrow).reshape(count, H, head_size)
    value_grad = jnp.einsum(
        "hqk,qhd->khd", state["prob_low"], context_grad, preferred_element_type=single
    )
    prob_grad = jnp.einsum(
        "qhd,khd->hqk", context_grad, state["vals"], preferred_element_type=single
    )
    prob = state["prob"]
    score_grad = (prob * (prob_grad - jnp.sum(prob_grad * prob, -1, keepdims=True))).astype(narrow)
    query_grad = (
        jnp.einsum("hqk,khd->qhd", score_grad, state["keys"], preferred_element_type=single) * scale
    )
    key_grad = (
        jnp.einsum("hqk,qhd->khd", score_grad, state["query"], preferred_element_type=single)
        * scale
    )
    mixed_grad = jnp.concatenate(
        [
            query_grad.reshape(count, width),
            key_grad.reshape(count, width),
            value_grad.reshape(count, width),
        ],
        1,
    ).astype(narrow)
    query_bias_grad = jnp.sum(mixed_grad[:, :width].astype(single), 0)
    value_bias_grad = jnp.sum(mixed_grad[:, 2 * width :].astype(single), 0)
    in_grad = jnp.einsum("td,tc->dc", state["x_low"], mixed_grad, preferred_element_type=single)
    resid_grad = first_grad + jnp.einsum(
        "tc,dc->td", mixed_grad, w_in, preferred_element_type=single
    )
    short_sum = jnp.sum(resid_grad.reshape(4, slot, width), 0)
    padded_sum = jnp.concatenate([short_sum, jnp.zeros((count - slot, width), single)], 0)
    table_grad = jnp.where(long_flag > 0, resid_grad, padded_sum)
    grads = (
        table_grad,
        in_grad,
        query_bias_grad,
        value_bias_grad,
        out_grad,
        out_bias_grad,
        gain_one_grad,
        shift_one_grad,
        up_grad,
        up_bias_grad,
        down_grad,
        down_bias_grad,
        gain_two_grad,
        shift_two_grad,
    )
    return (resid_grad, grads)


def slot_roles(bucket):
    long_slot = jnp.repeat(jnp.repeat(bucket, 2), 4) > 0
    slots = jnp.arange(long_slot.shape[0], dtype=jnp.int32)
    within = slots % 4
    odd_group = slots // 4 % 2
    query = jnp.where(long_slot, (within == 0) & (odd_group == 0), within % 2 == 0)
    passage = jnp.where(long_slot, (within == 0) & (odd_group == 1), within % 2 == 1)
    partner = jnp.where(long_slot, slots + 4, slots + 1)
    return (query, passage, partner)


def contrast(logits, query_rows, partner_rows, passage, pair_count):
    columns = jnp.arange(logits.shape[1], dtype=jnp.int32)
    masked = jnp.where(passage[None, :], logits, -1000000000.0)
    top = jnp.max(masked, -1, keepdims=True)
    raised = jnp.exp(masked - top)
    total = jnp.sum(raised, -1, keepdims=True)
    spread = top[:, 0] + jnp.log(total[:, 0])
    match = columns[None, :] == partner_rows[:, None]
    positive = jnp.sum(jnp.where(match, logits, 0.0), -1)
    row_terms = jnp.where(query_rows, spread - positive, 0.0)
    loss = jnp.sum(row_terms) / pair_count
    row_weight = jnp.where(query_rows, 1.0, 0.0) / pair_count
    logit_grad = (row_weight[:, None] * (raised / total - match.astype(single))).astype(narrow)
    return (loss, logit_grad, top[:, 0], total[:, 0], row_terms)


def local(
    tokens,
    lengths,
    bucket,
    position_table,
    in_projection,
    query_bias,
    value_bias,
    out_projection,
    out_bias,
    first_gain,
    first_shift,
    up_projection,
    up_bias,
    down_projection,
    down_bias,
    second_gain,
    second_shift,
):
    weights = (
        lax.all_gather(position_table, "fsdp", axis=1, tiled=True),
        lax.all_gather(in_projection, "fsdp", axis=0, tiled=True),
        lax.all_gather(query_bias, "fsdp", axis=0, tiled=True),
        lax.all_gather(value_bias, "fsdp", axis=0, tiled=True),
        lax.all_gather(out_projection, "fsdp", axis=0, tiled=True),
        lax.all_gather(out_bias, "fsdp", axis=0, tiled=True),
        lax.all_gather(first_gain, "fsdp", axis=0, tiled=True),
        lax.all_gather(first_shift, "fsdp", axis=0, tiled=True),
        lax.all_gather(up_projection, "fsdp", axis=0, tiled=True),
        lax.all_gather(up_bias, "fsdp", axis=0, tiled=True),
        lax.all_gather(down_projection, "fsdp", axis=0, tiled=True),
        lax.all_gather(down_bias, "fsdp", axis=0, tiled=True),
        lax.all_gather(second_gain, "fsdp", axis=0, tiled=True),
        lax.all_gather(second_shift, "fsdp", axis=0, tiled=True),
    )
    groups_dev = lengths.shape[0]
    width = tokens.shape[1]
    count = tokens.shape[0] // groups_dev
    device = lax.axis_index("dp") * lax.axis_size("fsdp") + lax.axis_index("fsdp")
    long_own = lax.dynamic_slice_in_dim(jnp.repeat(bucket, 2), device * groups_dev, groups_dev)
    blocks = tokens.reshape(groups_dev, count, width)
    pooled = lax.map(
        lambda item: group_pool(item[0], item[1], item[2], weights), (blocks, long_own, lengths)
    )
    pooled = pooled.reshape(groups_dev * 4, width)
    embedded, norm_back = jax.vjp(normalize_rows, pooled)
    embed_low = embedded.astype(narrow)
    every = lax.all_gather(embed_low, ("dp", "fsdp"), axis=0, tiled=True)
    query, passage, partner = slot_roles(bucket)
    pair_count = jnp.sum(4 - 3 * bucket).astype(single)
    rows = embed_low.shape[0]
    start = device * rows
    own_query = lax.dynamic_slice_in_dim(query, start, rows)
    own_partner = lax.dynamic_slice_in_dim(partner, start, rows)
    logits = jnp.einsum("id,jd->ij", embed_low, every, preferred_element_type=single) * 100.0
    part, logit_grad, own_top, own_total, own_terms = contrast(
        logits, own_query, own_partner, passage, pair_count
    )
    as_query = jnp.einsum("ij,jd->id", logit_grad, every, preferred_element_type=single) * 100.0
    loss = lax.psum(part, ("dp", "fsdp"))
    as_passage = (
        jnp.einsum("ij,id->jd", logit_grad, embed_low, preferred_element_type=single) * 100.0
    )
    embed_grad = as_query + lax.psum_scatter(
        as_passage, ("dp", "fsdp"), scatter_dimension=0, tiled=True
    )
    pooled_grad = norm_back(embed_grad)[0]
    weights_back = (
        lax.all_gather(position_table, "fsdp", axis=1, tiled=True),
        lax.all_gather(in_projection, "fsdp", axis=0, tiled=True),
        lax.all_gather(query_bias, "fsdp", axis=0, tiled=True),
        lax.all_gather(value_bias, "fsdp", axis=0, tiled=True),
        lax.all_gather(out_projection, "fsdp", axis=0, tiled=True),
        lax.all_gather(out_bias, "fsdp", axis=0, tiled=True),
        lax.all_gather(first_gain, "fsdp", axis=0, tiled=True),
        lax.all_gather(first_shift, "fsdp", axis=0, tiled=True),
        lax.all_gather(up_projection, "fsdp", axis=0, tiled=True),
        lax.all_gather(up_bias, "fsdp", axis=0, tiled=True),
        lax.all_gather(down_projection, "fsdp", axis=0, tiled=True),
        lax.all_gather(down_bias, "fsdp", axis=0, tiled=True),
        lax.all_gather(second_gain, "fsdp", axis=0, tiled=True),
        lax.all_gather(second_shift, "fsdp", axis=0, tiled=True),
    )
    empty = tuple((jnp.zeros(piece.shape, single) for piece in weights_back))

    def step(totals, item):
        resid_grad, grads = group_backward(item[0], item[1], item[2], item[3], weights_back)
        return (tuple((left + right for left, right in zip(totals, grads))), resid_grad)

    totals, token_grads = lax.scan(
        step, empty, (blocks, long_own, lengths, pooled_grad.reshape(groups_dev, 4, width))
    )
    owned = (
        lax.psum_scatter(totals[0], "fsdp", scatter_dimension=1, tiled=True),
        lax.psum_scatter(totals[1], "fsdp", scatter_dimension=0, tiled=True),
        lax.psum_scatter(totals[2], "fsdp", scatter_dimension=0, tiled=True),
        lax.psum_scatter(totals[3], "fsdp", scatter_dimension=0, tiled=True),
        lax.psum_scatter(totals[4], "fsdp", scatter_dimension=0, tiled=True),
        lax.psum_scatter(totals[5], "fsdp", scatter_dimension=0, tiled=True),
        lax.psum_scatter(totals[6], "fsdp", scatter_dimension=0, tiled=True),
        lax.psum_scatter(totals[7], "fsdp", scatter_dimension=0, tiled=True),
        lax.psum_scatter(totals[8], "fsdp", scatter_dimension=0, tiled=True),
        lax.psum_scatter(totals[9], "fsdp", scatter_dimension=0, tiled=True),
        lax.psum_scatter(totals[10], "fsdp", scatter_dimension=0, tiled=True),
        lax.psum_scatter(totals[11], "fsdp", scatter_dimension=0, tiled=True),
        lax.psum_scatter(totals[12], "fsdp", scatter_dimension=0, tiled=True),
        lax.psum_scatter(totals[13], "fsdp", scatter_dimension=0, tiled=True),
    )
    summed = (
        lax.psum(owned[0].astype(jnp.bfloat16), "dp").astype(jnp.float32),
        lax.psum(owned[1].astype(jnp.bfloat16), "dp").astype(jnp.float32),
        lax.psum(owned[2].astype(jnp.bfloat16), "dp").astype(jnp.float32),
        lax.psum(owned[3].astype(jnp.bfloat16), "dp").astype(jnp.float32),
        lax.psum(owned[4].astype(jnp.bfloat16), "dp").astype(jnp.float32),
        lax.psum(owned[5].astype(jnp.bfloat16), "dp").astype(jnp.float32),
        lax.psum(owned[6].astype(jnp.bfloat16), "dp").astype(jnp.float32),
        lax.psum(owned[7].astype(jnp.bfloat16), "dp").astype(jnp.float32),
        lax.psum(owned[8].astype(jnp.bfloat16), "dp").astype(jnp.float32),
        lax.psum(owned[9].astype(jnp.bfloat16), "dp").astype(jnp.float32),
        lax.psum(owned[10].astype(jnp.bfloat16), "dp").astype(jnp.float32),
        lax.psum(owned[11].astype(jnp.bfloat16), "dp").astype(jnp.float32),
        lax.psum(owned[12].astype(jnp.bfloat16), "dp").astype(jnp.float32),
        lax.psum(owned[13].astype(jnp.bfloat16), "dp").astype(jnp.float32),
    )
    return (
        loss,
        pooled,
        token_grads.reshape(groups_dev * count, width),
        summed[0],
        summed[1],
        summed[2],
        summed[3],
        summed[4],
        summed[5],
        summed[6],
        summed[7],
        summed[8],
        summed[9],
        summed[10],
        summed[11],
        summed[12],
        summed[13],
    )


def solution(mesh):
    in_specs = (
        P(("dp", "fsdp"), None),
        P(("dp", "fsdp"), None),
        P(),
        P(None, "fsdp"),
        P("fsdp", None),
        P("fsdp"),
        P("fsdp"),
        P("fsdp", None),
        P("fsdp"),
        P("fsdp"),
        P("fsdp"),
        P("fsdp", None),
        P("fsdp"),
        P("fsdp", None),
        P("fsdp"),
        P("fsdp"),
        P("fsdp"),
    )
    out_specs = (
        P(),
        P(("dp", "fsdp"), None),
        P(("dp", "fsdp"), None),
        P(None, "fsdp"),
        P("fsdp", None),
        P("fsdp"),
        P("fsdp"),
        P("fsdp", None),
        P("fsdp"),
        P("fsdp"),
        P("fsdp"),
        P("fsdp", None),
        P("fsdp"),
        P("fsdp", None),
        P("fsdp"),
        P("fsdp"),
        P("fsdp"),
    )
    return jax.shard_map(local, mesh=mesh, in_specs=in_specs, out_specs=out_specs, check_vma=False)
```

profile of v0, /device:TPU:0, one launch (start us, length us, event | category | flops | bytes accessed | tf_op | source)
XLA Modules:
  0.0 1140.7 jit_solution(3936059608471681190)
XLA Ops:
  12.7 14.4 %all-gather = bf16[8,1,384]{2,1,0:T(2,128)(2,1)S(1)} all-gather(bf16[1,1,384]{2,1,0:T(2,128)(2,1)S(1)} %reshape.669), channel_id=1, replica_groups=mesh['dp'=4,'fsdp'=8] {'fsdp'}, dimensions={0}, use_global_device_ids=true | all-gather | bytes 6912 | tf_op jit(solution)/shard_map/all_gather | solution.py:262
  28.2 16.4 %all_gather.58 = bf16[512,768]{0,1:T(8,128)(2,1)S(1)} all-gather(bf16[512,96]{0,1:T(8,128)(2,1)} %param.24), channel_id=1, replica_groups=mesh['dp'=4,'fsdp'=8] {'fsdp'}, dimensions={1}, use_global_device_ids=true | all-gather | bytes 884736 | tf_op jit(solution)/shard_map/all_gather | solution.py:253
  55.0 28.9 %all-reduce.19 = (bf16[768]{0:T(1024)(128)(2,1)S(1)}, bf16[768]{0:T(1024)(128)(2,1)S(1)}, bf16[768]{0:T(1024)(128)(2,1)S(1)}, bf16[768]{0:T(1024)(128)(2,1)S(1)}...) all-reduce(bf16[768]{0:T(1024)(128)(2,1)S(1)} %dynamic-update-slice, ...), channel_id=1, replica_groups=mesh['dp'=4,'fsdp'=8] {'fsdp'}, use_global_device_ids=true, to_apply=%add.1 | all-reduce | flops 6144 | bytes 24576
  84.4 47.0 %all-gather.10.cloned.1.call-done = bf16[768,3072]{1,0:T(8,128)(2,1)} async-done(((bf16[96,3072]{1,0:T(8,128)(2,1)}), bf16[768,3072]{1,0:T(8,128)(2,1)}) %all-gather.10.cloned.1.call-update) | async-done | bytes 4718608 | tf_op jit(solution)/shard_map/all_gather | solution.py:261
  131.4 52.0 %all-gather.12.cloned.1.call-done = bf16[3072,768]{1,0:T(8,128)(2,1)} async-done(((bf16[384,768]{1,0:T(8,128)(2,1)}), bf16[3072,768]{1,0:T(8,128)(2,1)}) %all-gather.12.cloned.1.call-update) | async-done | bytes 4718608 | tf_op jit(solution)/shard_map/all_gather | solution.py:263
  183.5 92.1 %while.53 = (s32[]{:T(128)}, f32[2,4,768]{2,1,0:T(4,128)S(1)}, s32[2]{0:T(128)S(1)}, s32[2,4]{1,0:T(2,128)}, bf16[2,512,768]{2,1,0:T(8,128)(2,1)}, /*index=5*/bf...) while((s32[]{:T(128)}, f32[2,4,768]{2,1,0:T(4,128)S(1)}, ...), condition=%wide.region_8.9_spmd, body=%wide.region_0.8_spmd.sunk | while | flops 8210919424 | bytes 87838120 | solution.py:274
  187.1 4.5 fusion.307
  192.7 7.6 fusion.311
  200.3 5.9 fusion.312
  207.5 20.8 %fusion.314 = (f32[512]{0:T(512)S(1)}, f32[512,768]{1,0:T(8,128)S(1)}) fusion(f32[768]{0:T(1024)S(1)} %convert_element_type.649, bf16[3072,768]{1,0:T(8,128)(2,1)} %get-tuple-element.1578, bf16[768,3072]{1,0:T(8,128)(2,1)} %get-tuple-element.1576, f32[3072]{0:T(1024)S(1)} %convert_element_type.650, f32[512,768]{1,0:T(8,128)S(1)} %get-tuple-element.1437, ...), kind=kOutput, calls=%fused_computation.300.clone.1 | convolution fusion | flops 4940365312 | bytes 12610560 | tf_op jit(solution)/shard_map/while/body/eval_jaxpr/dot_general | solution.py:80
  233.1 4.5 fusion.307
  238.6 7.6 fusion.311
  246.2 5.9 fusion.312
  253.5 20.8 %fusion.314 = (f32[512]{0:T(512)S(1)}, f32[512,768]{1,0:T(8,128)S(1)}) fusion(f32[768]{0:T(1024)S(1)} %convert_element_type.649, bf16[3072,768]{1,0:T(8,128)(2,1)} %get-tuple-element.1578, bf16[768,3072]{1,0:T(8,128)(2,1)} %get-tuple-element.1576, f32[3072]{0:T(1024)S(1)} %convert_element_type.650, f32[512,768]{1,0:T(8,128)S(1)} %get-tuple-element.1437, ...), kind=kOutput, calls=%fused_computation.300.clone.1 | convolution fusion | flops 4940365312 | bytes 12610560 | tf_op jit(solution)/shard_map/while/body/eval_jaxpr/dot_general | solution.py:80
  275.9 40.8 %all_gather.72 = bf16[256,768]{1,0:T(8,128)(2,1)S(1)} all-gather(bf16[8,768]{1,0:T(8,128)(2,1)S(1)} %multiply_convert_fusion.4), channel_id=1, replica_groups=mesh['dp'=4,'fsdp'=8] {'dp','fsdp'}, dimensions={0}, use_global_device_ids=true | all-gather | bytes 405504 | tf_op jit(solution)/shard_map/all_gather | solution.py:280
  319.5 93.4 %reduce-scatter.7.cloned.1.call-done = f32[8,768]{1,0:T(8,128)} async-done(((f32[256,768]{1,0:T(8,128)}), f32[8,768]{1,0:T(8,128)}) %reduce-scatter.7.cloned.1.call-update) | async-done | bytes 24592 | tf_op jit(solution)/shard_map/reduce_scatter | solution.py:296
  414.1 271.1 %while.54 = (s32[]{:T(128)}, f32[512,768]{1,0:T(8,128)}, f32[768,2304]{1,0:T(8,128)}, f32[768]{0:T(1024)}, f32[768]{0:T(1024)}, /*index=5*/f32[768,768]{1,0:T(8,...) while((s32[]{:T(128)}, f32[512,768]{1,0:T(8,128)}, ...), condition=%wide.region_41.42_spmd.clone, body=%wide.region_18.41_spmd.clone.sunk | while | flops 24424308736 | bytes 558224768 | solution.py:322
  427.0 4.5 fusion.349
  434.4 10.3 fusion.353
  444.7 5.9 fusion.354
  452.1 19.7 %multiply_convert_fusion.12 = (bf16[512,3072]{1,0:T(8,128)(2,1)S(1)}, f32[512,3072]{1,0:T(8,128)}, f32[512,3072]{1,0:T(8,128)}) fusion(f32[3072]{0:T(1024)S(1)} %convert_element_type.678, bf16[768,3072]{1,0:T(8,128)(2,1)} %get-tuple-element.1690, f32[512,768]{1,0:T(8,128)S(1)} %get-tuple-element.1481, f32[768]{0:T(1024)S(1)} %convert_element_type.679, ...), kind=kOutput, calls=%fused_computation.134.clone.1 | convolution fusion | flops 2521694208 | bytes 22042624 | tf_op jit(solution)/shard_map/while/body/eval_jaxpr/dot_general | solution.py:78
  471.8 2.8 fusion.357
  477.4 8.7 convert_reduce_fusion.11
  486.2 3.2 multiply_reduce_fusion.23
  494.3 7.0 fusion.361
  501.6 2.2 select_add_fusion.27
  503.8 6.3 select_add_fusion.30
  510.2 5.2 select_add_fusion.32
  515.5 5.8 multiply_reduce_fusion.24
  521.3 6.9 multiply_convert_fusion.13
  529.4 2.0 multiply_convert_fusion.14
  533.1 2.1 bitcast_dynamic-update-slice_fusion.2
  539.6 7.0 select_add_fusion.25
  552.8 4.5 fusion.349
  560.2 10.3 fusion.353
  570.5 5.9 fusion.354
  577.8 19.8 %multiply_convert_fusion.12 = (bf16[512,3072]{1,0:T(8,128)(2,1)S(1)}, f32[512,3072]{1,0:T(8,128)}, f32[512,3072]{1,0:T(8,128)}) fusion(f32[3072]{0:T(1024)S(1)} %convert_element_type.678, bf16[768,3072]{1,0:T(8,128)(2,1)} %get-tuple-element.1690, f32[512,768]{1,0:T(8,128)S(1)} %get-tuple-element.1481, f32[768]{0:T(1024)S(1)} %convert_element_type.679, ...), kind=kOutput, calls=%fused_computation.134.clone.1 | convolution fusion | flops 2521694208 | bytes 22042624 | tf_op jit(solution)/shard_map/while/body/eval_jaxpr/dot_general | solution.py:78
  597.7 2.8 fusion.357
  603.3 8.5 convert_reduce_fusion.11
  611.8 3.1 multiply_reduce_fusion.23
  620.0 7.0 fusion.361
  627.2 4.1 select_add_fusion.27
  631.3 8.8 select_add_fusion.30
  640.1 8.3 select_add_fusion.32
  648.4 5.8 multiply_reduce_fusion.24
  654.2 6.9 multiply_convert_fusion.13
  662.4 2.0 multiply_convert_fusion.14
  666.1 2.1 bitcast_dynamic-update-slice_fusion.2
  670.1 2.9 select_add_fusion.24
  673.2 9.0 select_add_fusion.25
  685.2 3.0 copy.95
  691.1 32.5 %reduce-scatter.9.cloned.1.call-done = f32[512,96]{0,1:T(8,128)} async-done(((f32[512,768]{0,1:T(8,128)}), f32[512,96]{0,1:T(8,128)}) %reduce-scatter.9.cloned.1.call-update) | async-done | bytes 196624 | tf_op jit(solution)/shard_map/reduce_scatter | solution.py:326
  725.3 35.2 %reduce-scatter.13.cloned.1.call-done = f32[96,768]{1,0:T(8,128)} async-done(((f32[768,768]{1,0:T(8,128)}), f32[96,768]{1,0:T(8,128)}) %reduce-scatter.13.cloned.1.call-update) | async-done | bytes 294928 | tf_op jit(solution)/shard_map/reduce_scatter | solution.py:330
  762.1 77.2 %reduce-scatter.11.cloned.1.call-done = f32[96,2304]{1,0:T(8,128)} async-done(((f32[768,2304]{1,0:T(8,128)}), f32[96,2304]{1,0:T(8,128)}) %reduce-scatter.11.cloned.1.call-update) | async-done | bytes 884752 | tf_op jit(solution)/shard_map/reduce_scatter | solution.py:327
  841.3 98.2 %reduce-scatter.15.cloned.1.call-done = f32[96,3072]{1,0:T(8,128)} async-done(((f32[768,3072]{1,0:T(8,128)}), f32[96,3072]{1,0:T(8,128)}) %reduce-scatter.15.cloned.1.call-update) | async-done | bytes 1179664 | tf_op jit(solution)/shard_map/reduce_scatter | solution.py:334
  939.6 2.2 convert_element_type.467
  941.7 97.9 %reduce-scatter.17.cloned.1.call-done = f32[384,768]{1,0:T(8,128)} async-done(((f32[3072,768]{1,0:T(8,128)}), f32[384,768]{1,0:T(8,128)}) %reduce-scatter.17.cloned.1.call-update) | async-done | bytes 1179664 | tf_op jit(solution)/shard_map/reduce_scatter | solution.py:336
  1039.6 2.1 convert_element_type.471
  1043.7 38.0 %psum.105 = f32[]{:T(128)} all-reduce(f32[]{:T(128)S(6)} %div.163), channel_id=1, replica_groups=mesh['dp'=4,'fsdp'=8] {'dp','fsdp'}, use_global_device_ids=true, to_apply=%region_15.16 | all-reduce | flops 1 | bytes 8 | tf_op jit(solution)/shard_map/psum | solution.py:292
  1081.8 27.3 %all-reduce.18 = (bf16[768]{0:T(1024)(128)(2,1)S(1)}, bf16[768]{0:T(1024)(128)(2,1)S(1)}, bf16[768]{0:T(1024)(128)(2,1)S(1)}, bf16[768]{0:T(1024)(128)(2,1)S(1)}...) all-reduce(f32[768]{0:T(1024)S(1)} %copy-done.59, ...), channel_id=5, replica_groups=mesh['dp'=4,'fsdp'=8] {'fsdp'}, use_global_device_ids=true, to_apply=%region_46.47.clone | all-reduce | flops 9216 | bytes 55296
  1109.8 9.9 all-reduce.20
  1127.6 2.0 convert_element_type.454
  1129.6 2.2 convert_element_type.468
  1131.7 2.2 convert_element_type.472
  (574 shorter events, 95.0 us)
Async XLA Ops:
  7.2 77.2 %all-gather.8.cloned.1.call-start = ((), (), s32[]{:S(2)}) async-start(), calls=%async_computation.7 | async-start | bytes 1327104 | tf_op jit(solution)/shard_map/all_gather | solution.py:257
  7.9 76.5 %all-gather.6.cloned.1.call-start = ((), (), s32[]{:S(2)}) async-start(), calls=%async_computation.6 | async-start | bytes 3981312 | tf_op jit(solution)/shard_map/all_gather | solution.py:254
  8.7 122.8 %all-gather.10.cloned.1.call-start = ((), (), s32[]{:S(2)}) async-start(), calls=%async_computation.8 | async-start | bytes 5308416 | tf_op jit(solution)/shard_map/all_gather | solution.py:261
  9.4 174.1 %all-gather.12.cloned.1.call-start = ((), (), s32[]{:S(2)}) async-start(), calls=%async_computation.9 | async-start | bytes 5308416 | tf_op jit(solution)/shard_map/all_gather | solution.py:263
  10.0 402.9 %reduce-scatter.7.cloned.1.call-start = ((), (), s32[]{:S(2)}) async-start(), calls=%async_computation.10 | async-start | bytes 811008 | tf_op jit(solution)/shard_map/reduce_scatter | solution.py:296
  183.5 133.3 %copy-start.63 = (pred[256]{0:T(512)(128)(4,1)S(1)}, pred[256]{0:T(512)(128)(4,1)}, u32[]{:S(2)}) copy-start(pred[256]{0:T(512)(128)(4,1)} %get-tuple-element.1090) | copy-start | bytes 772
  183.5 133.6 %copy-start.64 = (s32[8]{0:T(128)S(1)}, s32[8]{0:T(128)}, u32[]{:S(2)}) copy-start(s32[8]{0:T(128)} %dynamic_slice.57) | copy-start | bytes 100
  183.5 133.8 %copy-start.65 = (pred[256]{0:T(512)(128)(4,1)S(1)}, pred[256]{0:T(512)(128)(4,1)}, u32[]{:S(2)}) copy-start(pred[256]{0:T(512)(128)(4,1)} %get-tuple-element.1089) | copy-start | bytes 772
  275.6 43.8 %copy-start.72 = (s32[2]{0:T(128)}, s32[2]{0:T(128)S(1)}, u32[]{:S(2)}) copy-start(s32[2]{0:T(128)S(1)} %get-tuple-element.1769) | copy-start | bytes 28
  275.7 138.4 %copy-start.29 = (f32[8,768]{1,0:T(8,128)}, f32[8,768]{1,0:T(8,128)S(1)}, u32[]{:S(2)}) copy-start(f32[8,768]{1,0:T(8,128)S(1)} %reshape.640) | copy-start | bytes 73732
  319.3 404.4 %reduce-scatter.9.cloned.1.call-start = ((), (), s32[]{:S(2)}) async-start(), calls=%async_computation.11 | async-start | bytes 1769472 | tf_op jit(solution)/shard_map/reduce_scatter | solution.py:326
  421.2 10.4 copy-start.25
  421.2 10.4 copy-start.30
  421.2 10.4 copy-start.32
  421.2 10.4 copy-start.40
  421.2 10.4 copy-start.42
  421.3 53.7 %copy-start.27 = (f32[2,4,768]{2,1,0:T(4,128)}, f32[2,4,768]{2,1,0:T(4,128)S(1)}, u32[]{:S(2)}) copy-start(f32[2,4,768]{2,1,0:T(4,128)S(1)} %get-tuple-element.1679) | copy-start | bytes 73732 | tf_op jit(solution)/shard_map/while
  427.0 23.7 %copy-start.4 = (bf16[512,768]{1,0:T(8,128)(2,1)}, bf16[512,768]{1,0:T(8,128)(2,1)S(1)}, u32[]{:S(2)}) copy-start(bf16[512,768]{1,0:T(8,128)(2,1)S(1)} %bitcast_select_fusion.5) | copy-start | bytes 2359300 | tf_op jit(solution)/shard_map/while
  434.4 10.3 copy-start.17
  450.7 21.1 %copy-start.15 = (bf16[12,64,512]{2,1,0:T(8,128)(2,1)}, bf16[12,64,512]{2,1,0:T(8,128)(2,1)S(1)}, u32[]{:S(2)}) copy-start(bf16[12,64,512]{2,1,0:T(8,128)(2,1)S(1)} %fusion.354) | copy-start | bytes 2359300 | tf_op jit(solution)/shard_map/while
  450.7 21.0 %slice-start.5 = ((s8[4718592]{0:T(1024)(128)(4,1)}), s8[4194304]{0:T(1024)(128)(4,1)S(1)}, s32[]{:S(2)}) async-start(s8[4718592]{0:T(1024)(128)(4,1)} %bitcast.258), calls=%async_computation.22 | async-start | bytes 8388608 | tf_op jit(solution)/shard_map/while
  452.0 19.7 %copy-start.60 = (f32[768]{0:T(1024)S(1)}, f32[768]{0:T(1024)}, u32[]{:S(2)}) copy-start(f32[768]{0:T(1024)} %convert_element_type.680) | copy-start | bytes 9220 | tf_op jit(solution)/shard_map/while
  452.1 19.7 %slice-start.6 = ((s8[4718592]{0:T(1024)(128)(4,1)}), s8[524288]{0:T(1024)(128)(4,1)S(1)}, s32[]{:S(2)}) async-start(s8[4718592]{0:T(1024)(128)(4,1)} %bitcast.258), calls=%async_computation.23 | async-start | bytes 1048576 | tf_op jit(solution)/shard_map/while
  476.5 9.7 slice-start.3
  490.0 11.3 copy-start.46
  490.1 11.3 copy-start.48
  491.4 9.9 copy-start.50
  491.4 9.9 copy-start.52
  503.8 11.6 %slice-start = ((s8[12582912]{0:T(1024)(128)(4,1)}), s8[4194304]{0:T(1024)(128)(4,1)S(1)}, s32[]{:S(2)}) async-start(s8[12582912]{0:T(1024)(128)(4,1)} %bitcast.233), calls=%async_computation.17 | async-start | bytes 8388608 | tf_op jit(solution)/shard_map/while
  503.8 11.6 %slice-start.1 = ((s8[12582912]{0:T(1024)(128)(4,1)}), s8[4194304]{0:T(1024)(128)(4,1)S(1)}, s32[]{:S(2)}) async-start(s8[12582912]{0:T(1024)(128)(4,1)} %bitcast.233), calls=%async_computation.18 | async-start | bytes 8388608 | tf_op jit(solution)/shard_map/while
  547.0 10.4 copy-start.25
  547.0 10.4 copy-start.30
  547.0 10.4 copy-start.32
  547.0 10.4 copy-start.40
  547.0 10.4 copy-start.42
  547.0 53.8 %copy-start.27 = (f32[2,4,768]{2,1,0:T(4,128)}, f32[2,4,768]{2,1,0:T(4,128)S(1)}, u32[]{:S(2)}) copy-start(f32[2,4,768]{2,1,0:T(4,128)S(1)} %get-tuple-element.1679) | copy-start | bytes 73732 | tf_op jit(solution)/shard_map/while
  552.8 23.7 %copy-start.4 = (bf16[512,768]{1,0:T(8,128)(2,1)}, bf16[512,768]{1,0:T(8,128)(2,1)S(1)}, u32[]{:S(2)}) copy-start(bf16[512,768]{1,0:T(8,128)(2,1)S(1)} %bitcast_select_fusion.5) | copy-start | bytes 2359300 | tf_op jit(solution)/shard_map/while
  560.2 10.3 copy-start.17
  576.5 21.2 %copy-start.15 = (bf16[12,64,512]{2,1,0:T(8,128)(2,1)}, bf16[12,64,512]{2,1,0:T(8,128)(2,1)S(1)}, u32[]{:S(2)}) copy-start(bf16[12,64,512]{2,1,0:T(8,128)(2,1)S(1)} %fusion.354) | copy-start | bytes 2359300 | tf_op jit(solution)/shard_map/while
  576.5 21.1 %slice-start.5 = ((s8[4718592]{0:T(1024)(128)(4,1)}), s8[4194304]{0:T(1024)(128)(4,1)S(1)}, s32[]{:S(2)}) async-start(s8[4718592]{0:T(1024)(128)(4,1)} %bitcast.258), calls=%async_computation.22 | async-start | bytes 8388608 | tf_op jit(solution)/shard_map/while
  577.8 19.8 %copy-start.60 = (f32[768]{0:T(1024)S(1)}, f32[768]{0:T(1024)}, u32[]{:S(2)}) copy-start(f32[768]{0:T(1024)} %convert_element_type.680) | copy-start | bytes 9220 | tf_op jit(solution)/shard_map/while
  577.8 19.8 %slice-start.6 = ((s8[4718592]{0:T(1024)(128)(4,1)}), s8[524288]{0:T(1024)(128)(4,1)S(1)}, s32[]{:S(2)}) async-start(s8[4718592]{0:T(1024)(128)(4,1)} %bitcast.258), calls=%async_computation.23 | async-start | bytes 1048576 | tf_op jit(solution)/shard_map/while
  602.3 9.5 slice-start.3
  615.7 11.2 copy-start.46
  615.7 11.2 copy-start.48
  617.0 9.9 copy-start.50
  617.1 9.9 copy-start.52
  631.2 17.1 %slice-start = ((s8[12582912]{0:T(1024)(128)(4,1)}), s8[4194304]{0:T(1024)(128)(4,1)S(1)}, s32[]{:S(2)}) async-start(s8[12582912]{0:T(1024)(128)(4,1)} %bitcast.233), calls=%async_computation.17 | async-start | bytes 8388608 | tf_op jit(solution)/shard_map/while
  631.3 17.1 %slice-start.1 = ((s8[12582912]{0:T(1024)(128)(4,1)}), s8[4194304]{0:T(1024)(128)(4,1)S(1)}, s32[]{:S(2)}) async-start(s8[12582912]{0:T(1024)(128)(4,1)} %bitcast.233), calls=%async_computation.18 | async-start | bytes 8388608 | tf_op jit(solution)/shard_map/while
  673.0 9.1 copy-start.26
  673.0 9.1 copy-start.28
  673.0 9.1 copy-start.31
  673.1 9.1 copy-start.33
  673.1 9.1 copy-start.35
  673.1 9.1 copy-start.37
  673.1 9.1 copy-start.39
  673.1 9.1 copy-start.41
  688.3 72.2 %reduce-scatter.13.cloned.1.call-start = ((), (), s32[]{:S(2)}) async-start(), calls=%async_computation.13 | async-start | bytes 2654208 | tf_op jit(solution)/shard_map/reduce_scatter | solution.py:330
  689.0 150.3 %reduce-scatter.11.cloned.1.call-start = ((), (), s32[]{:S(2)}) async-start(), calls=%async_computation.12 | async-start | bytes 7962624 | tf_op jit(solution)/shard_map/reduce_scatter | solution.py:327
  689.8 249.8 %reduce-scatter.15.cloned.1.call-start = ((), (), s32[]{:S(2)}) async-start(), calls=%async_computation.14 | async-start | bytes 10616832 | tf_op jit(solution)/shard_map/reduce_scatter | solution.py:334
  690.5 349.1 %reduce-scatter.17.cloned.1.call-start = ((), (), s32[]{:S(2)}) async-start(), calls=%async_computation.15 | async-start | bytes 10616832 | tf_op jit(solution)/shard_map/reduce_scatter | solution.py:336
  691.1 390.7 %copy-start.56 = (f32[768]{0:T(1024)S(1)}, f32[768]{0:T(1024)}, u32[]{:S(2)}) copy-start(f32[768]{0:T(1024)} %get-tuple-element.676) | copy-start | bytes 9220
  691.1 390.7 %copy-start.59 = (f32[768]{0:T(1024)S(1)}, f32[768]{0:T(1024)}, u32[]{:S(2)}) copy-start(f32[768]{0:T(1024)} %get-tuple-element.675) | copy-start | bytes 9220
  691.1 433.3 %all-reduce.24.cloned.1.call-start = ((), (), s32[]{:S(2)}) async-start(), calls=%async_computation.16 | async-start | bytes 3735552 | tf_op jit(solution)/shard_map/psum | solution.py:342
  (100 other events, 518.2 us)
Sparse Core Ops, SparseCore 0:
  9.7 26.1 all-gather.7
  37.5 41.4 all-gather.5
  80.7 50.6 all-gather.9
  132.9 50.5 all-gather.11
  319.4 93.4 reduce-scatter.6
  688.4 35.2 reduce-scatter.8
  726.0 34.4 reduce-scatter.12
  762.8 76.4 reduce-scatter.10
  841.7 97.8 reduce-scatter.14
  941.7 97.8 reduce-scatter.16
  1044.4 65.6 all-reduce.23
where the time goes:
time: 1150 us; the launch traced here: 1140 us
  waiting for transfers between devices  539 us (47%)
  matrix products  288 us (25%)
  blocking collectives  176 us (15%)
  other arithmetic  59.9 us (5%)
  local copies, waits for them, and re-layouts  44.6 us (4%)
  between operations  17.8 us (2%)
  loops' own time  15.6 us (1%)
    reduce_scatter x1, waiting for transfers between devices, local(): lax.psum_scatter(totals[8], 'fsdp', scatter_dimension=0, tiled=True)  98.2 us
    reduce_scatter x1, waiting for transfers between devices, local(): lax.psum_scatter(totals[10], 'fsdp', scatter_dimension=0, tiled=True)  97.9 us
    reduce_scatter x1, waiting for transfers between devices, local(): lax.psum_scatter(as_passage, ('dp', 'fsdp'), scatter_dimension=0, tiled=T...  93.4 us
    reduce_scatter x1, waiting for transfers between devices, local(): lax.psum_scatter(totals[1], 'fsdp', scatter_dimension=0, tiled=True)  77.2 us
    unnamed x2, blocking collectives  56.2 us
    all_gather x1, waiting for transfers between devices, local(): lax.all_gather(down_projection, 'fsdp', axis=0, tiled=True)  52 us
    dot_general x4, matrix products, group_state(): jnp.dot(active, w_down, preferred_element_type=single)  47.3 us
    all_gather x1, waiting for transfers between devices, local(): lax.all_gather(up_projection, 'fsdp', axis=0, tiled=True)  47 us
  transfers between devices with their start and end apart: 11, of which 8 were waited for; matrix products, arithmetic and copies ran while one was open for 2% of the time, Pallas kernels for 0%

commit v1 on v0

v1 whole, which is shorter than its diff:
```python
import functools

import jax
import jax.numpy as jnp
from jax import lax
from jax.experimental import pallas as pl
from jax.experimental.pallas import tpu as pltpu
from jax.sharding import PartitionSpec as P

H = 12
narrow = jnp.bfloat16
single = jnp.float32
ANY = pl.ANY
VM = pltpu.VMEM
SM = pltpu.SMEM
LIMIT = 60 * 2**20


def dot(a, b):
    return lax.dot_general(a, b, (((1,), (0,)), ((), ())), preferred_element_type=single)


def dot_nt(a, b):
    return lax.dot_general(a, b, (((1,), (1,)), ((), ())), preferred_element_type=single)


def at(start, size):
    return pl.ds(pl.multiple_of(start, 128), size)


def gelu_pair(u):
    t = 1.0 / (1.0 + 0.23164189 * jnp.abs(u))
    e = jnp.exp(-0.5 * (u * u))
    tail = t * (
        0.127414796 + t * (-0.142248368 + t * (0.7107068705 + t * (-0.7265760135 + t * 0.5307027145)))
    )
    tail = tail * e
    phi = jnp.where(u < 0, tail, 1.0 - tail)
    return u * phi, phi + u * (e * 0.3989422804)


def norm_rows(value):
    mean = jnp.mean(value, -1, keepdims=True)
    centred = value - mean
    rstd = lax.rsqrt(jnp.mean(centred * centred, -1, keepdims=True) + 1e-06)
    return centred * rstd, rstd


def norm_back(grad, unit, rstd):
    one = jnp.mean(grad, -1, keepdims=True)
    two = jnp.mean(grad * unit, -1, keepdims=True)
    return rstd * (grad - one - unit * two)


def slot_lengths(lens, flag, g, along_rows, count, width):
    slot = count // 4
    shape = (count, width) if along_rows else (8, count)
    t = lax.broadcasted_iota(jnp.int32, shape, 0 if along_rows else 1)
    which = t // slot
    long = flag[g] > 0
    limit = jnp.where(which == 0, lens[g, 0], lens[g, 1])
    limit = jnp.where(which == 2, lens[g, 2], limit)
    limit = jnp.where(which == 3, lens[g, 3], limit)
    limit = jnp.where(long, lens[g, 0], limit)
    inside = jnp.where(long, t, t % slot)
    return which, inside < limit


def forward_kernel(
    sizes,
    lens, flag, vecs, tok, tab, w_in, w_out, w_up, w_down,
    x_o, mixed_o, prob_o, ctx_o, n1_o, r1_o, act_o, gp_o, n2_o, r2_o, pooled_o,
    v_in, v_out, v_up, v_down, tab_v, x_v, mixed, mask, pst, ctx, hid, hid_low, n_st, r1_v, r2_v, ast, gst, acc,
    in_sem, out_sem, p_sem, a_sem, g_sem,
):
    groups, count, width, ff = sizes
    rows = groups * count
    pairs = width // 128
    loads = [
        pltpu.make_async_copy(s, d, in_sem.at[i])
        for i, (s, d) in enumerate(
            ((tok, x_v), (tab, tab_v), (w_in, v_in), (w_out, v_out), (w_up, v_up), (w_down, v_down))
        )
    ]
    for c in loads:
        c.start()
    stores = []

    def store(src, dst):
        c = pltpu.make_async_copy(src, dst, out_sem.at[len(stores)])
        c.start()
        stores.append(c)

    def vec(i):
        return vecs[i : i + 1, :]

    loads[0].wait()
    loads[1].wait()
    slot = count // 4
    for g in range(groups):
        which_q, _ = slot_lengths(lens, flag, g, True, count, 128)
        which_k, live_k = slot_lengths(lens, flag, g, False, count, 128)
        long = flag[g] > 0
        wq = which_q[:, :1]
        open_ = live_k[:1] & (long | (wq == which_k[:1]))
        mask[g] = jnp.where(open_, 0.0, -1000000000.0).astype(single)
        for s in range(4):
            part = x_v[pl.ds(g * count + s * slot, slot), :].astype(single)
            place = jnp.where(long, tab_v[pl.ds(s * slot, slot), :].astype(single), tab_v[:slot, :].astype(single))
            both = part + place
            hid[pl.ds(g * count + s * slot, slot), :] = both
            x_v[pl.ds(g * count + s * slot, slot), :] = both.astype(narrow)
    store(x_v, x_o)

    loads[2].wait()
    for part in range(3):
        cols = pl.ds(part * width, width)

        def project(b, _, cols=cols, part=part):
            r = at(b * 256, 256)
            out = dot(x_v[r, :], v_in[:, cols])
            if part == 0:
                out = out + vec(0)
            if part == 2:
                out = out + vec(1)
            mixed[r, cols] = out.astype(narrow)
            return 0

        lax.fori_loop(0, rows // 256, project, 0)
    store(mixed, mixed_o)

    lane = lax.broadcasted_iota(jnp.int32, (count, 128), 1)
    half = (lane < 64, lane >= 64)

    def attend(i, _):
        g = i // pairs
        p = i % pairs
        s_ = i % 2
        r = at(g * count, count)

        @pl.when(i >= 2)
        def _():
            pltpu.make_async_copy(pst.at[s_], prob_o.at[i], p_sem.at[s_]).wait()

        q = mixed[r, at(p * 128, 128)]
        k = mixed[r, at(width + p * 128, 128)]
        v = mixed[r, at(2 * width + p * 128, 128)]
        zero = jnp.zeros_like(q)
        out = [None] * (count // 256)
        for h in range(2):
            qh = jnp.where(half[h], q, zero) * jnp.asarray(0.125, narrow)
            vh = jnp.where(half[h], v, zero)
            for b in range(count // 256):
                sc = dot_nt(qh[b * 256 : (b + 1) * 256], k) + mask[g, b * 256 : (b + 1) * 256, :]
                e = jnp.exp(sc - jnp.max(sc, -1, keepdims=True))
                low = (e * (1.0 / jnp.sum(e, -1, keepdims=True))).astype(narrow)
                pst[s_, h, b * 256 : (b + 1) * 256, :] = low
                o = dot(low, vh)
                out[b] = o if out[b] is None else out[b] + o
        for b in range(count // 256):
            ctx[at(g * count + b * 256, 256), at(p * 128, 128)] = out[b].astype(narrow)
        pltpu.make_async_copy(pst.at[s_], prob_o.at[i], p_sem.at[s_]).start()
        return 0

    n = groups * pairs
    lax.fori_loop(0, n, attend, 0)
    for i in range(max(n - 2, 0), n):
        pltpu.make_async_copy(pst.at[i % 2], prob_o.at[i], p_sem.at[i % 2]).wait()
    store(ctx, ctx_o)

    loads[3].wait()

    def first(b, _):
        r = at(b * 256, 256)
        total = hid[r, :] + dot(ctx[r, :], v_out[...]) + vec(2)
        unit, rstd = norm_rows(total)
        n_st[r, :] = unit
        r1_v[r, :] = jnp.broadcast_to(rstd, (256, 128))
        h = unit * vec(3) + vec(4)
        hid[r, :] = h
        hid_low[r, :] = h.astype(narrow)
        acc[r, :] = h + vec(5)
        return 0

    lax.fori_loop(0, rows // 256, first, 0)
    store(n_st, n1_o)
    store(r1_v, r1_o)

    loads[4].wait()
    loads[5].wait()
    wide = ff // width

    def act_copies(j, s_):
        return (
            pltpu.make_async_copy(ast.at[s_], act_o.at[j], a_sem.at[s_]),
            pltpu.make_async_copy(gst.at[s_], gp_o.at[j], g_sem.at[s_]),
        )

    for j in range(wide):
        s_ = j % 2
        if j >= 2:
            for c in act_copies(j - 2, s_):
                c.wait()
        cols = pl.ds(j * width, width)

        def feed(b, _, s_=s_, j=j, cols=cols):
            r = at(b * 256, 256)
            u = dot(hid_low[r, :], v_up[:, cols]) + vec(8 + j)
            a, d = gelu_pair(u)
            a = a.astype(narrow)
            ast[s_, r, :] = a
            gst[s_, r, :] = d.astype(narrow)
            acc[r, :] += dot(a, v_down[cols, :])
            return 0

        lax.fori_loop(0, rows // 256, feed, 0)
        for c in act_copies(j, s_):
            c.start()
    for j in range(max(wide - 2, 0), wide):
        for c in act_copies(j, j % 2):
            c.wait()

    stores[3].wait()
    for g in range(groups):
        _, live = slot_lengths(lens, flag, g, True, count, 128)
        sums = []
        for s in range(4):
            r = pl.ds(g * count + s * slot, slot)
            unit, rstd = norm_rows(acc[r, :])
            n_st[r, :] = unit
            r2_v[r, :] = jnp.broadcast_to(rstd, (slot, 128))
            out = unit * vec(6) + vec(7)
            keep = live[s * slot : (s + 1) * slot, :1]
            sums.append(jnp.sum(jnp.where(keep, out, 0.0), 0, keepdims=True))
        long = flag[g] > 0
        for s in range(4):
            div = jnp.maximum(lens[g, s], 1).astype(single)
            if s == 0:
                total = jnp.where(long, sums[0] + sums[1] + sums[2] + sums[3], sums[0])
            else:
                total = jnp.where(long, 0.0, sums[s])
            pooled_o[4 * g + s : 4 * g + s + 1, :] = total / div
    store(n_st, n2_o)
    store(r2_v, r2_o)
    for i, c in enumerate(stores):
        if i != 3:
            c.wait()


def backward_kernel(
    sizes,
    lens, flag, vecs, pg, w_in, w_out, w_up, w_down, x_i, mixed_i, prob_i, ctx_i, n1_i, r1_i, act_i, gp_i, n2_i, r2_i,
    tok_o, gin_o, gout_o, gup_o, gdown_o, gtab_o, gvec_o,
    v_in, v_out, v_up, v_down, x_v, mixed, ctx, n1, n2, r1_v, r2_v, ast, gst, pst, low, low_t, hid_t, up_low, grad, dctx, gst_a, gst_b, gsmall,
    in_sem, a_sem, p_sem, o_sem, b_sem,
):
    groups, count, width, ff = sizes
    rows = groups * count
    pairs = width // 128
    slot = count // 4
    wide = ff // width
    blocks = rows // 256
    loads = [
        pltpu.make_async_copy(s, d, in_sem.at[i])
        for i, (s, d) in enumerate(
            (
                (n2_i, n2), (r2_i, r2_v), (n1_i, n1), (w_down, v_down), (w_up, v_up), (r1_i, r1_v), (ctx_i, ctx),
                (w_out, v_out), (mixed_i, mixed), (x_i, x_v), (w_in, v_in),
            )
        )
    ]
    (l_n2, l_r2, l_n1, l_down, l_up, l_r1, l_ctx, l_wout, l_mixed, l_x, l_win) = loads

    def act_loads(j):
        return (
            pltpu.make_async_copy(act_i.at[j], ast.at[j % 2], a_sem.at[j % 2]),
            pltpu.make_async_copy(gp_i.at[j], gst.at[j % 2], a_sem.at[2 + j % 2]),
        )

    def prob_load(i, s_):
        return pltpu.make_async_copy(prob_i.at[i], pst.at[s_], p_sem.at[s_])

    l_n2.start()
    l_r2.start()
    for c in act_loads(0):
        c.start()
    for c in loads[2:5]:
        c.start()
    for c in act_loads(1):
        c.start()
    for c in loads[5:]:
        c.start()
    prob_load(0, 0).start()
    prob_load(1, 1).start()

    def vec(i):
        return vecs[i : i + 1, :]

    stores = []

    def store(src, dst):
        c = pltpu.make_async_copy(src, dst, o_sem.at[len(stores)])
        c.start()
        stores.append(c)

    l_n2.wait()
    l_r2.wait()
    gain_sum = jnp.zeros((1, width), single)
    shift_sum = jnp.zeros((1, width), single)
    bias_sum = jnp.zeros((1, width), single)
    for g in range(groups):
        _, live = slot_lengths(lens, flag, g, True, count, 128)
        long = flag[g] > 0
        for s in range(4):
            r = pl.ds(g * count + s * slot, slot)
            mine = pg[4 * g + s : 4 * g + s + 1, :] / jnp.maximum(lens[g, s], 1).astype(single)
            first = pg[4 * g : 4 * g + 1, :] / jnp.maximum(lens[g, 0], 1).astype(single)
            row = jnp.where(long, first, mine)
            keep = live[s * slot : (s + 1) * slot, :1]
            d = jnp.where(keep, row, 0.0)
            unit = n2[r, :]
            gain_sum = gain_sum + jnp.sum(d * unit, 0, keepdims=True)
            shift_sum = shift_sum + jnp.sum(d, 0, keepdims=True)
            back = norm_back(d * vec(6), unit, r2_v[r, :1])
            grad[r, :] = back
            lowered = back.astype(narrow)
            low[r, :] = lowered
            bias_sum = bias_sum + jnp.sum(lowered.astype(single), 0, keepdims=True)
            low_t[:, r] = lowered.T
    gsmall[...] = jnp.zeros_like(gsmall)
    gsmall[6:7, :] = gain_sum
    gsmall[7:8, :] = shift_sum
    gsmall[5:6, :] = bias_sum
    l_n1.wait()
    for b in range(rows // slot):
        r = pl.ds(b * slot, slot)
        hid_t[:, r] = (n1[r, :] * vec(3) + vec(4)).astype(narrow).T

    l_down.wait()
    l_up.wait()

    for j in range(wide):
        s_ = j % 2
        cols = pl.ds(j * width, width)
        for c in act_loads(j):
            c.wait()
        if j >= 1:
            pltpu.make_async_copy(gst_a, gdown_o.at[:, pl.ds((j - 1) * width, width)], b_sem.at[0]).wait()
            pltpu.make_async_copy(gst_b, gup_o.at[:, pl.ds((j - 1) * width, width)], b_sem.at[1]).wait()

        def feed(b, total, s_=s_, cols=cols):
            r = at(b * 256, 256)
            up = (dot_nt(low[r, :], v_down[cols, :]) * gst[s_, r, :].astype(single)).astype(narrow)
            up_low[r, :] = up
            grad[r, :] += dot_nt(up, v_up[:, cols])
            return total + jnp.sum(up.astype(single), 0, keepdims=True)

        gsmall[8 + j : 9 + j, :] = lax.fori_loop(0, blocks, feed, jnp.zeros((1, width), single))

        def weigh(b, _, s_=s_):
            r = at(b * 256, 256)
            gst_a[r, :] = dot(low_t[r, :], ast[s_]).astype(narrow)
            gst_b[r, :] = dot(hid_t[r, :], up_low[...]).astype(narrow)
            return 0

        lax.fori_loop(0, width // 256, weigh, 0)
        pltpu.make_async_copy(gst_a, gdown_o.at[:, cols], b_sem.at[0]).start()
        pltpu.make_async_copy(gst_b, gup_o.at[:, cols], b_sem.at[1]).start()
        if j + 2 < wide:
            for c in act_loads(j + 2):
                c.start()

    l_r1.wait()
    l_ctx.wait()
    l_wout.wait()
    gain_sum = jnp.zeros((1, width), single)
    shift_sum = jnp.zeros((1, width), single)
    bias_sum = jnp.zeros((1, width), single)
    for b in range(rows // slot):
        r = pl.ds(b * slot, slot)
        d = grad[r, :]
        unit = n1[r, :]
        gain_sum = gain_sum + jnp.sum(d * unit, 0, keepdims=True)
        shift_sum = shift_sum + jnp.sum(d, 0, keepdims=True)
        back = norm_back(d * vec(3), unit, r1_v[r, :1])
        grad[r, :] = back
        lowered = back.astype(narrow)
        low[r, :] = lowered
        bias_sum = bias_sum + jnp.sum(lowered.astype(single), 0, keepdims=True)
        hid_t[:, r] = ctx[r, :].T
    gsmall[3:4, :] = gain_sum
    gsmall[4:5, :] = shift_sum
    gsmall[2:3, :] = bias_sum
    last = pl.ds((wide - 1) * width, width)
    pltpu.make_async_copy(gst_a, gdown_o.at[:, last], b_sem.at[0]).wait()
    pltpu.make_async_copy(gst_b, gup_o.at[:, last], b_sem.at[1]).wait()

    def out_weigh(b, _):
        r = at(b * 256, 256)
        gst_a[r, :] = dot(hid_t[r, :], low[...]).astype(narrow)
        return 0

    lax.fori_loop(0, width // 256, out_weigh, 0)
    store(gst_a, gout_o)

    def context_back(b, _):
        r = at(b * 256, 256)
        dctx[r, :] = dot_nt(low[r, :], v_out[...]).astype(narrow)
        return 0

    lax.fori_loop(0, blocks, context_back, 0)

    l_mixed.wait()
    lane = lax.broadcasted_iota(jnp.int32, (count, 128), 1)
    half = (lane < 64, lane >= 64)
    scale = jnp.asarray(0.125, narrow)
    n = groups * pairs

    def attend(i, _):
        g = i // pairs
        p = i % pairs
        s_ = i % 2
        r = at(g * count, count)
        prob_load(i, s_).wait()
        c_q = at(p * 128, 128)
        c_k = at(width + p * 128, 128)
        c_v = at(2 * width + p * 128, 128)
        q = mixed[r, c_q] * scale
        k = mixed[r, c_k]
        v = mixed[r, c_v]
        dc = dctx[r, c_q]
        c = ctx[r, c_q]
        q_t = q.T
        dc_t = dc.T
        zero = jnp.zeros_like(q)
        prod = dc.astype(single) * c.astype(single)
        dq = [None] * (count // 256)
        dk_t = []
        dv_t = []
        for h in range(2):
            dch = jnp.where(half[h], dc, zero)
            kh = jnp.where(half[h], k, zero)
            d = jnp.sum(jnp.where(half[h], prod, 0.0), -1, keepdims=True)
            dkh = None
            dvh = None
            for b in range(count // 256):
                rb = slice(b * 256, (b + 1) * 256)
                prob = pst[s_, h, rb, :]
                dp = dot_nt(dch[rb], v)
                ds = (prob.astype(single) * (dp - d[rb])).astype(narrow)
                o = dot(ds, kh)
                dq[b] = o if dq[b] is None else dq[b] + o
                hr = slice(h * 64, (h + 1) * 64)
                one = dot(q_t[hr, rb], ds)
                two = dot(dc_t[hr, rb], prob)
                dkh = one if dkh is None else dkh + one
                dvh = two if dvh is None else dvh + two
            dk_t.append(dkh)
            dv_t.append(dvh)
        for b in range(count // 256):
            mixed[at(g * count + b * 256, 256), c_q] = (dq[b] * 0.125).astype(narrow)
        mixed[r, c_k] = jnp.concatenate(dk_t, 0).T.astype(narrow)
        mixed[r, c_v] = jnp.concatenate(dv_t, 0).T.astype(narrow)

        @pl.when(i + 2 < n)
        def _():
            prob_load(i + 2, s_).start()

        return 0

    lax.fori_loop(0, n, attend, 0)

    l_x.wait()
    l_win.wait()
    for b in range(rows // slot):
        r = pl.ds(b * slot, slot)
        hid_t[:, r] = x_v[r, :].T
    stores[0].wait()

    def bias(b, total):
        r = at(b * 256, 256)
        return (
            total[0] + jnp.sum(mixed[r, :width].astype(single), 0, keepdims=True),
            total[1] + jnp.sum(mixed[r, 2 * width :].astype(single), 0, keepdims=True),
        )

    zero_row = jnp.zeros((1, width), single)
    q_sum, v_sum = lax.fori_loop(0, blocks, bias, (zero_row, zero_row))
    gsmall[0:1, :] = q_sum
    gsmall[1:2, :] = v_sum
    store(gsmall, gvec_o)
    for part in range(3):
        cols = pl.ds(part * width, width)
        buf = gst_a if part % 2 == 0 else gst_b
        if part == 2:
            pltpu.make_async_copy(gst_a, gin_o.at[:, pl.ds(0, width)], b_sem.at[0]).wait()

        def in_weigh(b, _, cols=cols, buf=buf):
            r = at(b * 256, 256)
            buf[r, :] = dot(hid_t[r, :], mixed[:, cols]).astype(narrow)
            return 0

        lax.fori_loop(0, width // 256, in_weigh, 0)
        pltpu.make_async_copy(buf, gin_o.at[:, cols], b_sem.at[part % 2]).start()

    def token_back(b, _):
        r = at(b * 256, 256)
        grad[r, :] += dot_nt(mixed[r, :], v_in[...])
        return 0

    lax.fori_loop(0, blocks, token_back, 0)
    store(grad, tok_o)
    for s in range(4):
        total = None
        for g in range(groups):
            long = flag[g] > 0
            r = pl.ds(g * count + s * slot, slot)
            if s == 0:
                other = grad[r, :]
                for o in range(1, 4):
                    other = other + grad[pl.ds(g * count + o * slot, slot), :]
                piece = jnp.where(long, grad[r, :], other)
            else:
                piece = jnp.where(long, grad[r, :], 0.0)
            total = piece if total is None else total + piece
        up_low[:, s * slot : (s + 1) * slot] = jnp.zeros_like(up_low[:, s * slot : (s + 1) * slot])
        up_low[:width, s * slot : (s + 1) * slot] = total.T.astype(narrow)
    store(up_low.at[pl.ds(0, width), pl.ds(0, count)], gtab_o)
    pltpu.make_async_copy(gst_b, gin_o.at[:, pl.ds(width, width)], b_sem.at[1]).wait()
    pltpu.make_async_copy(gst_a, gin_o.at[:, pl.ds(2 * width, width)], b_sem.at[0]).wait()
    for c in stores[1:]:
        c.wait()


def shapes_of(groups, count, width, ff):
    rows = groups * count
    pairs = width // 128
    wide = ff // width
    return dict(
        x=((rows, width), narrow),
        mixed=((rows, 3 * width), narrow),
        prob=((groups * pairs, 2, count, count), narrow),
        ctx=((rows, width), narrow),
        n1=((rows, width), single),
        r1=((rows, 128), single),
        act=((wide, rows, width), narrow),
        gp=((wide, rows, width), narrow),
        n2=((rows, width), single),
        r2=((rows, 128), single),
    )


def run_forward(groups, count, width, ff, lens, flag, vecs, tok, tab, weights):
    rows = groups * count
    saved = shapes_of(groups, count, width, ff)
    outs = [jax.ShapeDtypeStruct(*v) for v in saved.values()]
    outs.append(jax.ShapeDtypeStruct((groups * 4, width), single))
    spec_any = pl.BlockSpec(memory_space=ANY)
    spec_v = pl.BlockSpec(memory_space=VM)
    spec_s = pl.BlockSpec(memory_space=SM)
    dma = pltpu.SemaphoreType.DMA
    return pl.pallas_call(
        functools.partial(forward_kernel, (groups, count, width, ff)),
        out_shape=outs,
        in_specs=[spec_s, spec_s, spec_v] + [spec_any] * 6,
        out_specs=[spec_any] * 10 + [spec_v],
        scratch_shapes=[
            VM((width, 3 * width), narrow),
            VM((width, width), narrow),
            VM((width, ff), narrow),
            VM((ff, width), narrow),
            VM((count, width), narrow),
            VM((rows, width), narrow),
            VM((rows, 3 * width), narrow),
            VM((groups, count, count), single),
            VM((2, 2, count, count), narrow),
            VM((rows, width), narrow),
            VM((rows, width), single),
            VM((rows, width), narrow),
            VM((rows, width), single),
            VM((rows, 128), single),
            VM((rows, 128), single),
            VM((2, rows, width), narrow),
            VM((2, rows, width), narrow),
            VM((rows, width), single),
            dma((6,)), dma((8,)), dma((2,)), dma((2,)), dma((2,)),
        ],
        compiler_params=pltpu.CompilerParams(vmem_limit_bytes=LIMIT),
        cost_estimate=pl.CostEstimate(flops=2 * rows * width * (4 * width + 2 * ff), bytes_accessed=80 * 2**20, transcendentals=10**7),
        name="encoder_forward",
    )(lens, flag, vecs, tok, tab, *weights)


def run_backward(groups, count, width, ff, lens, flag, vecs, pooled_grad, weights, saved):
    rows = groups * count
    spec_any = pl.BlockSpec(memory_space=ANY)
    spec_v = pl.BlockSpec(memory_space=VM)
    spec_s = pl.BlockSpec(memory_space=SM)
    dma = pltpu.SemaphoreType.DMA
    return pl.pallas_call(
        functools.partial(backward_kernel, (groups, count, width, ff)),
        out_shape=[
            jax.ShapeDtypeStruct((rows, width), single),
            jax.ShapeDtypeStruct((width, 3 * width), narrow),
            jax.ShapeDtypeStruct((width, width), narrow),
            jax.ShapeDtypeStruct((width, ff), narrow),
            jax.ShapeDtypeStruct((width, ff), narrow),
            jax.ShapeDtypeStruct((width, count), narrow),
            jax.ShapeDtypeStruct((16, width), single),
        ],
        in_specs=[spec_s, spec_s, spec_v, spec_v] + [spec_any] * 14,
        out_specs=[spec_any] * 7,
        scratch_shapes=[
            VM((width, 3 * width), narrow),
            VM((width, width), narrow),
            VM((width, ff), narrow),
            VM((ff, width), narrow),
            VM((rows, width), narrow),
            VM((rows, 3 * width), narrow),
            VM((rows, width), narrow),
            VM((rows, width), single),
            VM((rows, width), single),
            VM((rows, 128), single),
            VM((rows, 128), single),
            VM((2, rows, width), narrow),
            VM((2, rows, width), narrow),
            VM((2, 2, count, count), narrow),
            VM((rows, width), narrow),
            VM((width, rows), narrow),
            VM((width, rows), narrow),
            VM((rows, width), narrow),
            VM((rows, width), single),
            VM((rows, width), narrow),
            VM((width, width), narrow),
            VM((width, width), narrow),
            VM((16, width), single),
            dma((11,)), dma((4,)), dma((2,)), dma((4,)), dma((2,)),
        ],
        compiler_params=pltpu.CompilerParams(vmem_limit_bytes=LIMIT),
        cost_estimate=pl.CostEstimate(flops=4 * rows * width * (4 * width + 2 * ff), bytes_accessed=100 * 2**20, transcendentals=0),
        name="encoder_backward",
    )(lens, flag, vecs, pooled_grad, *weights, *saved)


def normalize_rows(pooled):
    return pooled * lax.rsqrt(jnp.sum(pooled * pooled, -1, keepdims=True) + 1e-06)


def slot_roles(bucket):
    long_slot = jnp.repeat(jnp.repeat(bucket, 2), 4) > 0
    slots = jnp.arange(long_slot.shape[0], dtype=jnp.int32)
    within = slots % 4
    odd_group = slots // 4 % 2
    query = jnp.where(long_slot, (within == 0) & (odd_group == 0), within % 2 == 0)
    passage = jnp.where(long_slot, (within == 0) & (odd_group == 1), within % 2 == 1)
    partner = jnp.where(long_slot, slots + 4, slots + 1)
    return (query, passage, partner)


def contrast(every, own, start, rows, bucket):
    query, passage, partner = slot_roles(bucket)
    pair_count = jnp.sum(4 - 3 * bucket).astype(single)
    logits = jnp.einsum("id,jd->ij", every, every, preferred_element_type=single) * 100.0
    columns = jnp.arange(logits.shape[1], dtype=jnp.int32)
    masked = jnp.where(passage[None, :], logits, -1000000000.0)
    top = jnp.max(masked, -1, keepdims=True)
    raised = jnp.exp(masked - top)
    total = jnp.sum(raised, -1, keepdims=True)
    spread = top[:, 0] + jnp.log(total[:, 0])
    match = columns[None, :] == partner[:, None]
    positive = jnp.sum(jnp.where(match, logits, 0.0), -1)
    loss = jnp.sum(jnp.where(query, spread - positive, 0.0)) / pair_count
    row_weight = jnp.where(query, 1.0, 0.0) / pair_count
    logit_grad = (row_weight[:, None] * (raised / total - match.astype(single))).astype(narrow)
    by_row = lax.dynamic_slice_in_dim(logit_grad, start, rows, 0)
    by_column = lax.dynamic_slice_in_dim(logit_grad, start, rows, 1)
    both = jnp.dot(by_row, every, preferred_element_type=single) + jnp.einsum(
        "ij,id->jd", by_column, every, preferred_element_type=single
    )
    return loss, both * 100.0


def gather_weights(tab, w_in, w_out, w_up, w_down, small):
    gat = lambda a: lax.all_gather(a, "fsdp", axis=0, tiled=True)
    return lax.all_gather(tab, "fsdp", axis=1, tiled=True), gat(w_in), gat(w_out), gat(w_up), gat(w_down), gat(small)


def reduce_all(grads, small):
    done = []
    for a, axis in grads:
        part = lax.psum_scatter(a.astype(single), "fsdp", scatter_dimension=axis, tiled=True)
        done.append(lax.psum(part.astype(narrow), "dp").astype(single))
    return done, lax.psum(small, ("dp", "fsdp"))


def local(
    tokens, lengths, bucket, position_table, in_projection, query_bias, value_bias, out_projection, out_bias,
    first_gain, first_shift, up_projection, up_bias, down_projection, down_bias, second_gain, second_shift,
):
    groups = lengths.shape[0]
    width = tokens.shape[1]
    count = tokens.shape[0] // groups
    shards = lax.axis_size("fsdp")
    ff = up_projection.shape[1]
    fs = lax.axis_index("fsdp")
    device = lax.axis_index("dp") * shards + fs
    small_parts = (query_bias, value_bias, out_bias, first_gain, first_shift, down_bias, second_gain, second_shift)
    piece = query_bias.shape[0]
    wide_piece = up_bias.shape[0]
    small = jnp.concatenate(small_parts + (up_bias,))[None, :]
    table, w_in, w_out, w_up, w_down, small_all = gather_weights(
        position_table, in_projection, out_projection, up_projection, down_projection, small
    )
    heads = small_all[:, : 8 * piece].reshape(shards, 8, piece).transpose(1, 0, 2).reshape(8, width)
    vecs = jnp.concatenate(
        [heads, small_all[:, 8 * piece :].reshape(ff // width, width), jnp.zeros((8 - ff // width, width), narrow)]
    ).astype(single)
    flag = lax.dynamic_slice_in_dim(jnp.repeat(bucket, 2), device * groups, groups)
    weights = (w_in, w_out, w_up, w_down)
    *saved, pooled = run_forward(groups, count, width, ff, lengths, flag, vecs, tokens, table, weights)
    embedded, norm_grad = jax.vjp(normalize_rows, pooled)
    every = lax.all_gather(embedded.astype(narrow), ("dp", "fsdp"), axis=0, tiled=True)
    slots = groups * 4
    loss, embed_grad = contrast(every, embedded, device * slots, slots, bucket)
    pooled_grad = norm_grad(embed_grad)[0]
    tokens_grad, gin, gout, gup, gdown, gtab, gvec = run_backward(
        groups, count, width, ff, lengths, flag, vecs, pooled_grad, weights, saved
    )
    (gin, gout, gup, gdown, gtab), gvec = reduce_all(((gin, 0), (gout, 0), (gup, 0), (gdown, 1), (gtab, 0)), gvec)
    gdown = gdown.T
    gtab = gtab.T
    own = [lax.dynamic_slice_in_dim(gvec[i], fs * piece, piece) for i in range(8)]
    up_own = lax.dynamic_slice_in_dim(gvec[8 : 8 + ff // width].reshape(ff), fs * wide_piece, wide_piece)
    return (
        loss, pooled, tokens_grad, gtab, gin, own[0], own[1], gout, own[2], own[3], own[4], gup, up_own, gdown,
        own[5], own[6], own[7],
    )


def solution(mesh):
    rows = P(("dp", "fsdp"), None)
    vec = P("fsdp")
    mat = P("fsdp", None)
    in_specs = (rows, rows, P(), P(None, "fsdp"), mat, vec, vec, mat, vec, vec, vec, mat, vec, mat, vec, vec, vec)
    out_specs = (P(), rows, rows, P(None, "fsdp"), mat, vec, vec, mat, vec, vec, vec, mat, vec, mat, vec, vec, vec)
    return jax.shard_map(local, mesh=mesh, in_specs=in_specs, out_specs=out_specs, check_vma=False)
```

time: 1150 us -> 718 us (0.62)
  matrix products: 288 us -> 1.64 us
  Pallas kernels: 0 us -> 133 us
  waiting for transfers between devices: 539 us -> 413 us
  blocking collectives: 176 us -> 113 us
  other arithmetic: 59.9 us -> 26.3 us
  local copies, waits for them, and re-layouts: 44.6 us -> 13.6 us
  loops' own time: 15.6 us -> 0 us
    dot_general x49 -> x3, matrix products: 252 us -> 1.64 us  [the longest x1 1.04 us: contrast(): jnp.einsum('ij,id->jd', by_column, every, preferred_element_type=single)]
    reduce_scatter x6 -> x5, waiting for transfers between devices: 434 us -> 251 us  [reduce_all(): lax.psum_scatter(a.astype(single), 'fsdp', scatter_dimension=axis, tiled=...]
    pallas_call x0 -> x2, Pallas kernels: none -> 133 us  [the longest x1 75.1 us: run_backward(): pl.pallas_call(functools.partial(backward_kernel, (groups, count, width,...]
    unnamed x2 -> x0, blocking collectives: 56.2 us -> none
    sub x4 -> x0, matrix products: 35.8 us -> none  [group_state(): raised = jnp.exp(scores - top)]
    all_gather x4, waiting for transfers between devices: 99.1 us -> 129 us  [gather_weights(): gat = lambda a: lax.all_gather(a, 'fsdp', axis=0, tiled=True)]
    psum x1, waiting for transfers between devices: 0.01 us -> 27.8 us  [reduce_all(): done.append(lax.psum(part.astype(narrow), 'dp').astype(single))]
    convert_element_type x56 -> x8, other arithmetic: 43.9 us -> 17.2 us  [the longest x2 9.76 us: reduce_all(): a.astype(single)]
  transfers between devices with their start and end apart: 11 -> 10, of which waited for: 8 -> 9; matrix products, arithmetic and copies ran while one was open for 2% -> 4% of each run, Pallas kernels for 0% -> 0%
where the time goes in v1:
time: 718 us; the launch traced here: 717 us
  waiting for transfers between devices  413 us (58%)
  Pallas kernels  133 us (19%)
  blocking collectives  113 us (16%)
  other arithmetic  26.3 us (4%)
  between operations  16.8 us (2%)
  local copies, waits for them, and re-layouts  13.6 us (2%)
    reduce_scatter x5, waiting for transfers between devices, reduce_all(): lax.psum_scatter(a.astype(single), 'fsdp', scatter_dimension=axis, tiled=...  251 us
    all_gather x4, waiting for transfers between devices, gather_weights(): gat = lambda a: lax.all_gather(a, 'fsdp', axis=0, tiled=True)  129 us
    pallas_call x1, Pallas kernels, run_backward(): pl.pallas_call(functools.partial(backward_kernel, (groups, count, width,...  75.1 us
    pallas_call x1, Pallas kernels, run_forward(): pl.pallas_call(functools.partial(forward_kernel, (groups, count, width, f...  57.4 us
    all_gather x1, blocking collectives, local(): lax.all_gather(embedded.astype(narrow), ('dp', 'fsdp'), axis=0, tiled=True)  41.1 us
    psum x1, blocking collectives, reduce_all(): return (done, lax.psum(small, ('dp', 'fsdp')))  38.6 us
    psum x1, waiting for transfers between devices, reduce_all(): done.append(lax.psum(part.astype(narrow), 'dp').astype(single))  27.8 us
    all_gather x1, blocking collectives, gather_weights(): lax.all_gather(tab, 'fsdp', axis=1, tiled=True)  18 us
  transfers between devices with their start and end apart: 10, of which 9 were waited for; matrix products, arithmetic and copies ran while one was open for 4% of the time, Pallas kernels for 0%

profile of v1, /device:TPU:0, one launch (start us, length us, event | category | flops | bytes accessed | tf_op | source)
XLA Modules:
  0.0 717.3 jit_solution(12314551718223563039)
XLA Ops:
  7.2 0.7 all-gather.9.cloned.1.call-update
  7.9 0.0 all-gather.7.cloned.1.call-start
  8.0 0.7 all-gather.7.cloned.1.call-update
  8.7 0.7 all-gather.11.cloned.1.call-update
  9.4 0.0 all-gather.13.cloned.1.call-start
  9.5 0.5 all-gather.13.cloned.1.call-update
  10.0 0.0 reduce-scatter.6.cloned.1.call-start
  10.0 6.1 concatenate.6
  16.2 15.8 %all-gather.1 = bf16[8,1,1152]{2,1,0:T(2,128)(2,1)S(1)} all-gather(bf16[1,1,1152]{2,1,0:T(2,128)(2,1)S(1)} %reshape.221), channel_id=2, replica_groups=mesh['dp'=4,'fsdp'=8] {'fsdp'}, dimensions={0}, use_global_device_ids=true | all-gather | bytes 20736 | tf_op jit(solution)/shard_map/all_gather | solution.py:684
  32.0 0.7 broadcast_in_dim.51
  32.7 0.1 reshape.215
  32.8 0.1 broadcast_in_dim.52
  32.9 0.1 broadcast_in_dim.53
  33.0 1.3 subtract_reduce_fusion
  35.0 0.6 dynamic_slice.52.flag
  35.6 0.1 reshape.216
  35.7 0.1 reshape.217
  35.8 18.0 %all_gather.22 = bf16[512,768]{0,1:T(8,128)(2,1)S(1)} all-gather(bf16[512,96]{0,1:T(8,128)(2,1)} %param.20), channel_id=1, replica_groups=mesh['dp'=4,'fsdp'=8] {'fsdp'}, dimensions={1}, use_global_device_ids=true | all-gather | bytes 884736 | tf_op jit(solution)/shard_map/all_gather | solution.py:685
  53.8 1.2 copy.44.tab
  55.0 0.1 iota.84
  55.1 0.1 pad.2.clone
  55.2 0.7 maximum_convert_fusion.vecs
  55.9 24.7 %all-gather.7.cloned.1.call-done.w_in = bf16[768,2304]{1,0:T(8,128)(2,1)} async-done(((bf16[96,2304]{1,0:T(8,128)(2,1)}), bf16[768,2304]{1,0:T(8,128)(2,1)}) %all-gather.7.cloned.1.call-update) | async-done | bytes 3538960 | tf_op jit(solution)/shard_map/all_gather | solution.py:684
  80.6 52.2 %all-gather.11.cloned.1.call-done.w_up = bf16[768,3072]{1,0:T(8,128)(2,1)} async-done(((bf16[96,3072]{1,0:T(8,128)(2,1)}), bf16[768,3072]{1,0:T(8,128)(2,1)}) %all-gather.11.cloned.1.call-update) | async-done | bytes 4718608 | tf_op jit(solution)/shard_map/all_gather | solution.py:684
  132.7 52.0 %all-gather.13.cloned.1.call-done.w_down = bf16[3072,768]{1,0:T(8,128)(2,1)} async-done(((bf16[384,768]{1,0:T(8,128)(2,1)}), bf16[3072,768]{1,0:T(8,128)(2,1)}) %all-gather.13.cloned.1.call-update) | async-done | bytes 4718608 | tf_op jit(solution)/shard_map/all_gather | solution.py:684
  184.8 57.4 %encoder_forward.1 = (bf16[1024,768]{1,0:T(8,128)(2,1)}, bf16[1024,2304]{1,0:T(8,128)(2,1)}, bf16[12,2,512,512]{3,2,1,0:T(8,128)(2,1)}, bf16[1024,768]{1,0:T(8,1...) custom-call(s32[2,4]{1,0:T(2,128)} %lens.3, ...), custom_call_target="tpu_custom_call" | custom-call | flops 14495514624 | bytes 83886080 | tf_op jit(solution)/shard_map/encoder_forward/pallas_call | solution.py:562
  242.3 0.9 multiply_reduce_fusion.1
  243.2 0.8 multiply_convert_fusion.1
  244.0 41.1 %all_gather.27 = bf16[256,768]{1,0:T(8,128)(2,1)S(1)} all-gather(bf16[8,768]{1,0:T(8,128)(2,1)S(1)} %multiply_convert_fusion.1), channel_id=1, replica_groups=mesh['dp'=4,'fsdp'=8] {'dp','fsdp'}, dimensions={0}, use_global_device_ids=true | all-gather | bytes 405504 | tf_op jit(solution)/shard_map/all_gather | solution.py:722
  285.1 0.3 select_reduce_fusion.1
  285.4 0.1 fusion
  285.6 0.6 fusion.12
  286.2 0.1 multiply_convert_fusion
  286.3 0.3 fusion.1
  286.6 1.0 multiply_reduce_fusion
  287.7 0.7 add_add_fusion.pg
  288.4 75.1 %encoder_backward.1 = (f32[1024,768]{1,0:T(8,128)}, bf16[768,2304]{1,0:T(8,128)(2,1)}, bf16[768,768]{1,0:T(8,128)(2,1)}, bf16[768,3072]{1,0:T(8,128)(2,1)}, bf16...) custom-call(s32[2,4]{1,0:T(2,128)} %lens.3, s32[2]{0:T(128)} %dynamic_slice.52.flag, ...), custom_call_target="tpu_custom_call" | custom-call | flops 28991029248 | bytes 104857600 | tf_op jit(solution)/shard_map/encoder_backward/pallas_call | solution.py:600
  363.4 2.5 convert_element_type.61
  366.0 0.0 reduce-scatter.14.cloned.1.call-start
  366.0 7.3 %convert_element_type.72 = f32[768,3072]{1,0:T(8,128)} convert(bf16[768,3072]{1,0:T(8,128)(2,1)} %get-tuple-element.52) | non-fusion elementwise | flops 2359296 | bytes 14155776 | tf_op jit(solution)/shard_map/convert_element_type | solution.py:691
  373.3 0.0 reduce-scatter.10.cloned.1.call-start
  373.4 0.7 reduce-scatter.10.cloned.1.call-update
  374.1 0.7 reduce-scatter.8.cloned.1.call-update
  374.9 0.7 reduce-scatter.12.cloned.1.call-update
  375.6 0.0 all-reduce.3.cloned.1.call-start
  375.6 21.0 %reduce-scatter.6.cloned.1.call-done = f32[96,512]{1,0:T(8,128)} async-done(((f32[768,512]{1,0:T(8,128)}), f32[96,512]{1,0:T(8,128)}) %reduce-scatter.6.cloned.1.call-update) | async-done | bytes 196624 | tf_op jit(solution)/shard_map/reduce_scatter | solution.py:691
  396.6 1.6 convert_bitcast_fusion.1
  398.2 98.1 %reduce-scatter.14.cloned.1.call-done = f32[768,384]{1,0:T(8,128)} async-done(((f32[768,3072]{1,0:T(8,128)}), f32[768,384]{1,0:T(8,128)}) %reduce-scatter.14.cloned.1.call-update) | async-done | bytes 1179664 | tf_op jit(solution)/shard_map/reduce_scatter | solution.py:691
  496.2 2.1 convert_bitcast_fusion
  498.4 32.0 %reduce-scatter.10.cloned.1.call-done = bf16[96,768]{1,0:T(8,128)(2,1)} async-done(((bf16[768,768]{1,0:T(8,128)(2,1)}), bf16[96,768]{1,0:T(8,128)(2,1)}) %reduce-scatter.10.cloned.1.call-update) | async-done | bytes 147472 | tf_op jit(solution)/shard_map/reduce_scatter | solution.py:691
  530.4 44.2 %reduce-scatter.8.cloned.1.call-done = bf16[96,2304]{1,0:T(8,128)(2,1)} async-done(((bf16[768,2304]{1,0:T(8,128)(2,1)}), bf16[96,2304]{1,0:T(8,128)(2,1)}) %reduce-scatter.8.cloned.1.call-update) | async-done | bytes 442384 | tf_op jit(solution)/shard_map/reduce_scatter | solution.py:691
  574.6 55.9 %reduce-scatter.12.cloned.1.call-done = bf16[96,3072]{1,0:T(8,128)(2,1)} async-done(((bf16[768,3072]{1,0:T(8,128)(2,1)}), bf16[96,3072]{1,0:T(8,128)(2,1)}) %reduce-scatter.12.cloned.1.call-update) | async-done | bytes 589840 | tf_op jit(solution)/shard_map/reduce_scatter | solution.py:691
  631.2 38.6 %psum.44 = f32[16,768]{1,0:T(8,128)S(1)} all-reduce(f32[16,768]{1,0:T(8,128)S(1)} %copy-done.2), channel_id=1, replica_groups=mesh['dp'=4,'fsdp'=8] {'dp','fsdp'}, use_global_device_ids=true, to_apply=%region_11.12 | all-reduce | flops 12288 | bytes 98304 | tf_op jit(solution)/shard_map/psum | solution.py:693
  669.8 0.7 dynamic_slice.65
  670.4 0.6 fusion.14
  671.0 0.6 fusion.16
  671.6 0.6 fusion.18
  672.2 0.6 fusion.20
  672.8 27.8 %all-reduce.3.cloned.1.call-done = (bf16[384,768]{0,1:T(8,128)(2,1)}, bf16[512,96]{0,1:T(8,128)(2,1)}, bf16[96,2304]{1,0:T(8,128)(2,1)}, bf16[96,768]{1,0:T(8,128)(2,1)}, bf16[96,3072]{1,0:T(8,128)(2,1)}) async-done(((bf16[384,768]{0,1:T(8,128)(2,1)}, bf16[512,96]{0,1:T(8,128)(2,1)}, bf16[96,2304]{1,0:T(8,128)(2,1)}, bf16[96,768]{1,0:T(8,128)(2,1)}, bf16[96,3072]{1,0:T(8,128)(2,1)}), ...) | async-done | bytes 1867792 | tf_op jit(solution)/shard_map/psum | solution.py:692
  700.6 1.6 transpose.24
  702.2 2.0 convert_element_type.65
  704.2 1.6 convert_element_type.68
  705.8 2.2 convert_element_type.71
  708.0 1.3 copy.45
  (30 shorter events, 0.3 us)
Async XLA Ops:
  7.2 48.7 %all-gather.9.cloned.1.call-start = ((), (), s32[]{:S(2)}) async-start(), calls=%async_computation.6 | async-start | bytes 1327104 | tf_op jit(solution)/shard_map/all_gather | solution.py:684
  7.9 72.7 %all-gather.7.cloned.1.call-start = ((), (), s32[]{:S(2)}) async-start(), calls=%async_computation.5 | async-start | bytes 3981312 | tf_op jit(solution)/shard_map/all_gather | solution.py:684
  8.7 124.1 %all-gather.11.cloned.1.call-start = ((), (), s32[]{:S(2)}) async-start(), calls=%async_computation.7 | async-start | bytes 5308416 | tf_op jit(solution)/shard_map/all_gather | solution.py:684
  9.4 175.4 %all-gather.13.cloned.1.call-start = ((), (), s32[]{:S(2)}) async-start(), calls=%async_computation.8 | async-start | bytes 5308416 | tf_op jit(solution)/shard_map/all_gather | solution.py:684
  10.0 386.6 %reduce-scatter.6.cloned.1.call-start = ((), (), s32[]{:S(2)}) async-start(), calls=%async_computation.9 | async-start | bytes 1769472 | tf_op jit(solution)/shard_map/reduce_scatter | solution.py:691
  242.2 45.4 %copy-start.1 = (f32[8,768]{1,0:T(8,128)S(1)}, f32[8,768]{1,0:T(8,128)}, u32[]{:S(2)}) copy-start(f32[8,768]{1,0:T(8,128)} %get-tuple-element.105) | copy-start | bytes 73732
  366.0 130.3 %reduce-scatter.14.cloned.1.call-start = ((), (), s32[]{:S(2)}) async-start(), calls=%async_computation.13 | async-start | bytes 10616832 | tf_op jit(solution)/shard_map/reduce_scatter | solution.py:691
  373.3 157.1 %reduce-scatter.10.cloned.1.call-start = ((), (), s32[]{:S(2)}) async-start(), calls=%async_computation.11 | async-start | bytes 1327104 | tf_op jit(solution)/shard_map/reduce_scatter | solution.py:691
  374.1 200.5 %reduce-scatter.8.cloned.1.call-start = ((), (), s32[]{:S(2)}) async-start(), calls=%async_computation.10 | async-start | bytes 3981312 | tf_op jit(solution)/shard_map/reduce_scatter | solution.py:691
  374.8 255.7 %reduce-scatter.12.cloned.1.call-start = ((), (), s32[]{:S(2)}) async-start(), calls=%async_computation.12 | async-start | bytes 5308416 | tf_op jit(solution)/shard_map/reduce_scatter | solution.py:691
  375.5 255.6 %copy-start.2 = (f32[16,768]{1,0:T(8,128)S(1)}, f32[16,768]{1,0:T(8,128)}, u32[]{:S(2)}) copy-start(f32[16,768]{1,0:T(8,128)} %get-tuple-element.49) | copy-start | bytes 147460
  375.6 325.0 %all-reduce.3.cloned.1.call-start = ((), (), s32[]{:S(2)}) async-start(), calls=%async_computation.14 | async-start | bytes 3735552 | tf_op jit(solution)/shard_map/psum | solution.py:692
  700.6 7.5 %copy-start = (bf16[384,768]{0,1:T(8,128)(2,1)S(1)}, bf16[384,768]{0,1:T(8,128)(2,1)}, u32[]{:S(2)}) copy-start(bf16[384,768]{0,1:T(8,128)(2,1)} %get-tuple-element.123) | copy-start | bytes 1769476
Sparse Core Ops, SparseCore 0:
  9.7 25.5 all-gather.8
  36.9 43.6 all-gather.6
  82.2 50.4 all-gather.10
  134.2 50.5 all-gather.12
  366.1 30.4 reduce-scatter.5
  398.8 97.4 reduce-scatter.13
  499.1 31.2 reduce-scatter.9
  532.7 41.8 reduce-scatter.7
  577.0 53.4 reduce-scatter.11
  635.0 65.5 all-reduce.2

commit v2 on v1

--- a/solution.py
+++ b/solution.py
@@ -251,7 +251,7 @@
     sizes,
     lens, flag, vecs, pg, w_in, w_out, w_up, w_down, x_i, mixed_i, prob_i, ctx_i, n1_i, r1_i, act_i, gp_i, n2_i, r2_i,
     tok_o, gin_o, gout_o, gup_o, gdown_o, gtab_o, gvec_o,
-    v_in, v_out, v_up, v_down, x_v, mixed, ctx, n1, n2, r1_v, r2_v, ast, gst, pst, low, low_t, hid_t, up_low, grad, dctx, gst_a, gst_b, gsmall,
+    v_in, v_out, v_up, v_down, x_v, mixed, ctx, n1, n2, r1_v, r2_v, ast, gst, pst, low, hid_t, up_low, grad, dctx, gst_a, gst_b, gsmall,
     in_sem, a_sem, p_sem, o_sem, b_sem,
 ):
     groups, count, width, ff = sizes
@@ -326,7 +326,6 @@
             lowered = back.astype(narrow)
             low[r, :] = lowered
             bias_sum = bias_sum + jnp.sum(lowered.astype(single), 0, keepdims=True)
-            low_t[:, r] = lowered.T
     gsmall[...] = jnp.zeros_like(gsmall)
     gsmall[6:7, :] = gain_sum
     gsmall[7:8, :] = shift_sum
@@ -345,7 +344,7 @@
         for c in act_loads(j):
             c.wait()
         if j >= 1:
-            pltpu.make_async_copy(gst_a, gdown_o.at[:, pl.ds((j - 1) * width, width)], b_sem.at[0]).wait()
+            pltpu.make_async_copy(gst_a, gdown_o.at[pl.ds((j - 1) * width, width), :], b_sem.at[0]).wait()
             pltpu.make_async_copy(gst_b, gup_o.at[:, pl.ds((j - 1) * width, width)], b_sem.at[1]).wait()
 
         def feed(b, total, s_=s_, cols=cols):
@@ -359,12 +358,12 @@
 
         def weigh(b, _, s_=s_):
             r = at(b * 256, 256)
-            gst_a[r, :] = dot(low_t[r, :], ast[s_]).astype(narrow)
+            gst_a[r, :] = dot(ast[s_, :, r].T, low[...]).astype(narrow)
             gst_b[r, :] = dot(hid_t[r, :], up_low[...]).astype(narrow)
             return 0
 
         lax.fori_loop(0, width // 256, weigh, 0)
-        pltpu.make_async_copy(gst_a, gdown_o.at[:, cols], b_sem.at[0]).start()
+        pltpu.make_async_copy(gst_a, gdown_o.at[cols, :], b_sem.at[0]).start()
         pltpu.make_async_copy(gst_b, gup_o.at[:, cols], b_sem.at[1]).start()
         if j + 2 < wide:
             for c in act_loads(j + 2):
@@ -392,7 +391,7 @@
     gsmall[4:5, :] = shift_sum
     gsmall[2:3, :] = bias_sum
     last = pl.ds((wide - 1) * width, width)
-    pltpu.make_async_copy(gst_a, gdown_o.at[:, last], b_sem.at[0]).wait()
+    pltpu.make_async_copy(gst_a, gdown_o.at[last, :], b_sem.at[0]).wait()
     pltpu.make_async_copy(gst_b, gup_o.at[:, last], b_sem.at[1]).wait()
 
     def out_weigh(b, _):
@@ -604,7 +603,7 @@
             jax.ShapeDtypeStruct((width, 3 * width), narrow),
             jax.ShapeDtypeStruct((width, width), narrow),
             jax.ShapeDtypeStruct((width, ff), narrow),
-            jax.ShapeDtypeStruct((width, ff), narrow),
+            jax.ShapeDtypeStruct((ff, width), narrow),
             jax.ShapeDtypeStruct((width, count), narrow),
             jax.ShapeDtypeStruct((16, width), single),
         ],
@@ -627,7 +626,6 @@
             VM((2, 2, count, count), narrow),
             VM((rows, width), narrow),
             VM((width, rows), narrow),
-            VM((width, rows), narrow),
             VM((rows, width), narrow),
             VM((rows, width), single),
             VM((rows, width), narrow),
@@ -680,6 +678,478 @@
     return loss, both * 100.0
 
 
+MESH = pl.DeviceIdType.MESH
+
+
+def place():
+    dp, fs = lax.axis_index("dp"), lax.axis_index("fsdp")
+    return dp % 2, dp // 2, fs // 2, fs % 2
+
+
+def device_at(x, y, z, c):
+    return (y * 2 + x, z * 2 + c)
+
+
+class Wires:
+    def __init__(self, send, recv):
+        self.send, self.recv, self.next, self.sent = send, recv, 0, []
+
+    def copy(self, src, dst, device):
+        i = self.next
+        self.next += 1
+        made = pltpu.make_async_remote_copy(
+            src_ref=src, dst_ref=dst, send_sem=self.send.at[i], recv_sem=self.recv.at[i],
+            device_id=device, device_id_type=MESH,
+        )
+        made.start()
+        self.sent.append(made)
+        return made
+
+    def finish(self):
+        for made in self.sent:
+            made.wait_send()
+
+
+def greet(devices):
+    barrier = pltpu.get_barrier_semaphore()
+    for d in devices:
+        pl.semaphore_signal(barrier, inc=1, device_id=d, device_id_type=MESH)
+    pl.semaphore_wait(barrier, len(devices))
+
+
+def neighbours(small_too):
+    x, y, z, c = place()
+    found = [device_at(1 - x, y, z, c), device_at(x, 1 - y, z, c), device_at(x, y, z, 1 - c)]
+    for k in (1, 2, 3):
+        found.append(device_at(x, y, (z + k) % 4, c))
+        if small_too:
+            found.append(device_at(x, y, (z + k) % 4, 1 - c))
+    return found
+
+
+class Gather:
+    def __init__(self, wires, shard, full, route):
+        self.w, self.shard, self.full, self.route = wires, shard, full, route
+        self.rows, self.cols = shard.shape
+        self.x, self.y, self.z, self.c = place()
+
+    def piece(self, ref, fs, a, b, part=None):
+        hr, hc = self.rows // 2, self.cols // 2
+        start = a * hr if fs is None else fs * self.rows + a * hr
+        if part is not None:
+            hr = hr // 2
+            start = start + part * hr
+        return ref.at[pl.ds(pl.multiple_of(start, 16), hr), pl.ds(pl.multiple_of(b * hc, 128), hc)]
+
+    def whole(self, fs):
+        return self.full.at[pl.ds(pl.multiple_of(fs * self.rows, 16), self.rows), :]
+
+    def start(self, local_sem):
+        x, y, z, c = self.x, self.y, self.z, self.c
+        mine = 2 * z + c
+        self.local = pltpu.make_async_copy(self.shard, self.whole(mine), local_sem)
+        self.local.start()
+        self.by_z = [
+            self.w.copy(self.piece(self.shard, None, x, y), self.piece(self.full, mine, x, y), device_at(x, y, (z + k) % 4, c))
+            for k in (1, 2, 3)
+        ]
+        self.by_core = [self.w.copy(self.shard, self.whole(mine), device_at(x, y, z, 1 - c))]
+
+    def plane(self):
+        x, y, z, c = self.x, self.y, self.z, self.c
+        self.by_x, self.by_y = [], []
+        for k in (1, 2, 3):
+            self.by_z[k - 1].wait_recv()
+            mine = self.piece(self.full, 2 * ((z - k) % 4) + c, x, y)
+            self.by_x.append(self.w.copy(mine, mine, device_at(1 - x, y, z, c)))
+            self.by_y.append(self.w.copy(mine, mine, device_at(x, 1 - y, z, c)))
+
+    def diagonal(self):
+        x, y, z, c = self.x, self.y, self.z, self.c
+        self.by_corner = []
+        for k in (1, 2, 3):
+            fs = 2 * ((z - k) % 4) + c
+            self.by_x[k - 1].wait_recv()
+            self.by_y[k - 1].wait_recv()
+            way = self.route[k - 1]
+            if way == "x":
+                got = self.piece(self.full, fs, 1 - x, y)
+                self.by_corner.append(self.w.copy(got, got, device_at(x, 1 - y, z, c)))
+            elif way == "y":
+                got = self.piece(self.full, fs, x, 1 - y)
+                self.by_corner.append(self.w.copy(got, got, device_at(1 - x, y, z, c)))
+            else:
+                got = self.piece(self.full, fs, 1 - x, y, 0)
+                self.by_corner.append(self.w.copy(got, got, device_at(x, 1 - y, z, c)))
+                got = self.piece(self.full, fs, x, 1 - y, 1)
+                self.by_corner.append(self.w.copy(got, got, device_at(1 - x, y, z, c)))
+
+    def core(self):
+        x, y, z, c = self.x, self.y, self.z, self.c
+        for made in self.by_corner:
+            made.wait_recv()
+        for k in (1, 2, 3):
+            fs = 2 * ((z - k) % 4) + c
+            self.by_core.append(self.w.copy(self.whole(fs), self.whole(fs), device_at(x, y, z, 1 - c)))
+
+    def finish(self):
+        for made in self.by_core:
+            made.wait_recv()
+        self.local.wait()
+
+
+ROUTES = (("x", "y", "x"), ("x", "y", "y"), ("x", "y", "x"), ("x", "y", "y"), ("x", "y", "both"))
+
+
+def gather_kernel(count, small, *refs):
+    shards, fulls = refs[:count], refs[count + 1 : 2 * count + 1]
+    small_all = refs[count]
+    send, recv, local_sems = refs[2 * count + 1 :]
+    x, y, z, c = place()
+    greet(neighbours(True))
+    wires = Wires(send, recv)
+    mine = 2 * z + c
+    keep = pltpu.make_async_copy(small, small_all.at[mine], local_sems.at[count])
+    keep.start()
+    little = [
+        wires.copy(small, small_all.at[mine], device_at(x, y, (z + k) % 4, (c + j) % 2))
+        for k in range(4)
+        for j in range(2)
+        if (k, j) != (0, 0)
+    ]
+    work = [Gather(wires, shards[i], fulls[i], ROUTES[i]) for i in range(count)]
+    for t in range(count + 3):
+        if t < count:
+            work[t].start(local_sems.at[t])
+        for stage, back in (("plane", 1), ("diagonal", 2), ("core", 3)):
+            if 0 <= t - back < count:
+                getattr(work[t - back], stage)()
+    for g in work:
+        g.finish()
+    for made in little:
+        made.wait_recv()
+    keep.wait()
+    wires.finish()
+
+
+def run_gather(small, shards):
+    count = len(shards)
+    n_small = 7
+    copies = n_small + sum(3 + 6 + len([w for w in r]) + ("both" in r) + 4 for r in ROUTES[:count])
+    spec = pl.BlockSpec(memory_space=ANY)
+    dma = pltpu.SemaphoreType.DMA
+    return pl.pallas_call(
+        functools.partial(gather_kernel, count),
+        out_shape=[jax.ShapeDtypeStruct((8,) + small.shape, small.dtype)]
+        + [jax.ShapeDtypeStruct((8 * s.shape[0], s.shape[1]), s.dtype) for s in shards],
+        in_specs=[spec] * (count + 1),
+        out_specs=[spec] * (count + 1),
+        scratch_shapes=[dma((copies,)), dma((copies,)), dma((count + 1,))],
+        compiler_params=pltpu.CompilerParams(collective_id=1, has_side_effects=True),
+        name="gather_weights",
+    )(small, *shards)
+
+
+class Reduce:
+    def __init__(self, wires, grad, own, from_core, b1x, b1y, b2x, b2y, from_z, final, sem):
+        self.w, self.grad, self.own, self.from_core = wires, grad, own, from_core
+        self.b1x, self.b1y, self.b2x, self.b2y, self.from_z, self.final, self.sem = b1x, b1y, b2x, b2y, from_z, final, sem
+        _, self.rows, self.cols = own.shape
+        self.x, self.y, self.z, self.c = place()
+
+    def rh(self, a):
+        return pl.ds(pl.multiple_of(a * (self.rows // 2), 16), self.rows // 2)
+
+    def ch(self, b):
+        return pl.ds(pl.multiple_of(b * (self.cols // 2), 128), self.cols // 2)
+
+    def add(self, zs, row0, rows, cols, other, step=48):
+        blocks = rows // step
+
+        def body(i, _):
+            zi = i // blocks
+            r = i % blocks * step
+            mine = (zs[0] + zi, pl.ds(pl.multiple_of(row0 + r, 16), step), cols)
+            theirs = other[zi, pl.ds(pl.multiple_of(r, 16), step), :]
+            self.own[mine] = (self.own[mine].astype(single) + theirs.astype(single)).astype(narrow)
+            return 0
+
+        lax.fori_loop(0, len(zs) * blocks, body, 0)
+
+    def start(self):
+        x, y, z, c = self.x, self.y, self.z, self.c
+        self.keep = pltpu.make_async_copy(self.grad.at[:, c], self.own, self.sem)
+        self.keep.start()
+        self.s0 = self.w.copy(self.grad.at[:, 1 - c], self.from_core, device_at(x, y, z, 1 - c))
+
+    def first(self):
+        x, y, z, c = self.x, self.y, self.z, self.c
+        self.keep.wait()
+        self.s0.wait_recv()
+        self.add((0, 1, 2, 3), 0, self.rows, slice(None), self.from_core)
+        lo, hi = pl.ds(0, 2), pl.ds(2, 2)
+        self.s1 = (
+            self.w.copy(self.own.at[lo, self.rh(1 - x), :], self.b1x, device_at(1 - x, y, z, c)),
+            self.w.copy(self.own.at[hi, :, self.ch(1 - y)], self.b1y, device_at(x, 1 - y, z, c)),
+        )
+
+    def second(self):
+        x, y, z, c = self.x, self.y, self.z, self.c
+        for s in self.s1:
+            s.wait_recv()
+        self.add((0, 1), x * (self.rows // 2), self.rows // 2, slice(None), self.b1x)
+        self.add((2, 3), 0, self.rows, self.ch(y), self.b1y)
+        lo, hi = pl.ds(0, 2), pl.ds(2, 2)
+        self.s2 = (
+            self.w.copy(self.own.at[lo, self.rh(x), self.ch(1 - y)], self.b2y, device_at(x, 1 - y, z, c)),
+            self.w.copy(self.own.at[hi, self.rh(1 - x), self.ch(y)], self.b2x, device_at(1 - x, y, z, c)),
+        )
+
+    def third(self):
+        x, y, z, c = self.x, self.y, self.z, self.c
+        for s in self.s2:
+            s.wait_recv()
+        self.add((0, 1), x * (self.rows // 2), self.rows // 2, self.ch(y), self.b2y)
+        self.add((2, 3), x * (self.rows // 2), self.rows // 2, self.ch(y), self.b2x)
+        self.s3 = [
+            self.w.copy(self.own.at[(z + k) % 4, self.rh(x), self.ch(y)], self.from_z.at[k - 1], device_at(x, y, (z + k) % 4, c))
+            for k in (1, 2, 3)
+        ]
+
+    def fourth(self):
+        x, y, z, c = self.x, self.y, self.z, self.c
+        for s in self.s3:
+            s.wait_recv()
+        half = self.rows // 2
+
+        def body(i, _):
+            r = pl.ds(pl.multiple_of(i * 48, 16), 48)
+            mine = pl.ds(pl.multiple_of(x * half + i * 48, 16), 48)
+            total = self.own[z, mine, self.ch(y)].astype(single)
+            for k in range(3):
+                total = total + self.from_z[k, r, :].astype(single)
+            self.final[mine, self.ch(y)] = total.astype(narrow)
+            return 0
+
+        lax.fori_loop(0, half // 48, body, 0)
+        mine = self.final.at[self.rh(x), self.ch(y)]
+        self.s4 = [
+            self.w.copy(mine, mine, device_at(1 - x, y, z, c)),
+            self.w.copy(mine, mine, device_at(x, 1 - y, z, c)),
+            self.w.copy(mine, mine, device_at(1 - x, 1 - y, z, c)),
+        ]
+
+    def finish(self, out):
+        for s in self.s4:
+            s.wait_recv()
+
+        def body(i, _):
+            r = pl.ds(pl.multiple_of(i * 48, 16), 48)
+            out[r, :] = self.final[r, :].astype(single)
+            return 0
+
+        lax.fori_loop(0, self.rows // 48, body, 0)
+
+
+class ReduceSmall:
+    def __init__(self, wires, total, got):
+        self.w, self.total, self.got = wires, total, got
+
+    def send(self, i, device):
+        return self.w.copy(self.total.at[i], self.got.at[i], device)
+
+    def start(self):
+        x, y, z, c = place()
+        self.s = self.send(0, device_at(x, y, z, 1 - c))
+
+    def step(self, i):
+        x, y, z, c = place()
+        self.s.wait_recv()
+        self.total[i + 1] = self.total[i] + self.got[i]
+        if i == 0:
+            self.s = self.send(1, device_at(1 - x, y, z, c))
+        elif i == 1:
+            self.s = self.send(2, device_at(x, 1 - y, z, c))
+        else:
+            self.last = [
+                self.w.copy(self.total.at[3], self.got.at[2 + k], device_at(x, y, (z + k) % 4, c)) for k in (1, 2, 3)
+            ]
+
+    def finish(self, out):
+        for s in self.last:
+            s.wait_recv()
+        x, y, z, c = place()
+        out[...] = jnp.zeros_like(out)
+        for i in range(4):
+            term = jnp.zeros_like(out)
+            for k in range(4):
+                part = self.total[3] if k == 0 else self.got[2 + k]
+                term = jnp.where((z - k + 4) % 4 == i, part, term)
+            out[...] = out[...] + term
+
+
+def reduce_kernel(count, small, *refs):
+    grads, outs, rest = refs[:count], refs[count : 2 * count + 1], refs[2 * count + 1 :]
+    total, got, send, recv, sems = rest[:5]
+    scratch = rest[5:]
+    x, y, z, c = place()
+    wires = Wires(send, recv)
+    greet(neighbours(False) + [device_at(1 - x, 1 - y, z, c)])
+    work = [Reduce(wires, grads[i], *scratch[8 * i : 8 * i + 8], sems.at[i]) for i in range(count)]
+    total[0] = small[...]
+    tiny = ReduceSmall(wires, total, got)
+    for w in work:
+        w.start()
+    tiny.start()
+    for t in range(count + 4):
+        for stage, back in (("first", 0), ("second", 1), ("third", 2), ("fourth", 3)):
+            if 0 <= t - back < count:
+                getattr(work[t - back], stage)()
+        if 0 <= t - 4 < count:
+            work[t - 4].finish(outs[t - 4])
+        if t < 3:
+            tiny.step(t)
+    tiny.finish(outs[count])
+    wires.finish()
+
+
+def run_reduce(grads, small):
+    count = len(grads)
+    spec = pl.BlockSpec(memory_space=ANY)
+    spec_v = pl.BlockSpec(memory_space=VM)
+    dma = pltpu.SemaphoreType.DMA
+    scratch = []
+    for g in grads:
+        _, _, r, k = g.shape
+        scratch += [
+            VM((4, r, k), narrow), VM((4, r, k), narrow), VM((2, r // 2, k), narrow), VM((2, r, k // 2), narrow),
+            VM((2, r // 2, k // 2), narrow), VM((2, r // 2, k // 2), narrow), VM((3, r // 2, k // 2), narrow),
+            VM((r, k), narrow),
+        ]
+    copies = 11 * count + 6
+    return pl.pallas_call(
+        functools.partial(reduce_kernel, count),
+        out_shape=[jax.ShapeDtypeStruct(g.shape[2:], single) for g in grads] + [jax.ShapeDtypeStruct(small.shape, single)],
+        in_specs=[spec_v] + [spec] * count,
+        out_specs=[spec_v] * (count + 1),
+        scratch_shapes=[
+            VM((4,) + small.shape, single), VM((6,) + small.shape, single), dma((copies,)), dma((copies,)), dma((count,)),
+        ] + scratch,
+        compiler_params=pltpu.CompilerParams(collective_id=2, has_side_effects=True, vmem_limit_bytes=LIMIT),
+        name="reduce_gradients",
+    )(small, *grads)
+
+
+def contrast_kernel(slots, buckets, bucket, pooled, loss_o, grad_o, mine, every, full, send, recv, sem):
+    x, y, z, c = place()
+    device = (y * 2 + x) * 8 + 2 * z + c
+    greet(neighbours(False))
+    wires = Wires(send, recv)
+    p = pooled[...]
+    scale = lax.rsqrt(jnp.sum(p * p, -1, keepdims=True) + 1e-06)
+    e = p * scale
+    width = e.shape[1]
+    hw = width // 2
+    mine[...] = jnp.concatenate([e[:, :hw], e[:, hw:]], 0).astype(narrow)
+
+    def slot_of(xx, yy, zz):
+        return (yy * 2 + xx) * 8 + 2 * zz + c
+
+    def block(xx, yy, zz):
+        return every.at[slot_of(xx, yy, zz)]
+
+    keep = pltpu.make_async_copy(mine, every.at[device], sem)
+    keep.start()
+    by_x = wires.copy(mine, block(x, y, z), device_at(1 - x, y, z, c))
+    by_y = [wires.copy(mine, block(x, y, z), device_at(x, 1 - y, z, c))]
+    by_z = [wires.copy(mine, block(x, y, z), device_at(x, y, (z + k) % 4, c)) for k in (1, 2, 3)]
+    by_x.wait_recv()
+    by_y.append(wires.copy(block(1 - x, y, z), block(1 - x, y, z), device_at(x, 1 - y, z, c)))
+    by_z += [wires.copy(block(1 - x, y, z), block(1 - x, y, z), device_at(x, y, (z + k) % 4, c)) for k in (1, 2, 3)]
+    for s in by_y:
+        s.wait_recv()
+    for xx in (x, 1 - x):
+        by_z += [
+            wires.copy(block(xx, 1 - y, z), block(xx, 1 - y, z), device_at(x, y, (z + k) % 4, c)) for k in (1, 2, 3)
+        ]
+    pair_size = 8
+
+    def long_of(shape, axis):
+        pair = lax.broadcasted_iota(jnp.int32, shape, axis) // pair_size
+        found = jnp.zeros(shape, jnp.int32)
+        for b in range(buckets):
+            found = jnp.where(pair == b, bucket[b], found)
+        return found > 0
+
+    def roles(shape, axis):
+        t = lax.broadcasted_iota(jnp.int32, shape, axis)
+        long = long_of(shape, axis)
+        within, odd = t % 4, t // 4 % 2
+        query = jnp.where(long, jnp.where((within == 0) & (odd == 0), 1, 0), jnp.where(within % 2 == 0, 1, 0))
+        passage = jnp.where(long, jnp.where((within == 0) & (odd == 1), 1, 0), jnp.where(within % 2 == 1, 1, 0))
+        return query > 0, passage > 0, jnp.where(long, t + 4, t + 1)
+
+    _, passage, _ = roles((8, slots), 1)
+    query, _, partner = roles((slots, 128), 0)
+    passage, query, partner = passage[:1], query[:, :1], partner[:, :1]
+    pair_count = jnp.zeros((), single)
+    for b in range(buckets):
+        pair_count = pair_count + (4 - 3 * bucket[b]).astype(single)
+    keep.wait()
+    for s in by_z:
+        s.wait_recv()
+    others = []
+    for yy in range(2):
+        for xx in range(2):
+            for zz in range(4):
+                others.append(wires.copy(block(xx, yy, zz), block(xx, yy, zz), device_at(x, y, z, 1 - c)))
+    for s in others:
+        s.wait_recv()
+    both = every[...].astype(single)
+    left = both[:, :8, :].reshape(slots, hw).astype(narrow)
+    right = both[:, 8:, :].reshape(slots, hw).astype(narrow)
+    logits = (dot_nt(left, left) + dot_nt(right, right)) * 100.0
+    masked = jnp.where(passage, logits, -1000000000.0)
+    top = jnp.max(masked, -1, keepdims=True)
+    raised = jnp.exp(masked - top)
+    total = jnp.sum(raised, -1, keepdims=True)
+    match = lax.broadcasted_iota(jnp.int32, (slots, slots), 1) == partner
+    positive = jnp.sum(jnp.where(match, logits, 0.0), -1, keepdims=True)
+    terms = jnp.where(query, top + jnp.log(total) - positive, 0.0)
+    loss = jnp.sum(terms, 0, keepdims=True) / pair_count
+    loss_o[...] = jnp.broadcast_to(loss, loss_o.shape)
+    weight = jnp.where(query, 1.0, 0.0) / pair_count
+    logit_grad = weight * (raised / total - jnp.where(match, 1.0, 0.0))
+    by_row = logit_grad.astype(narrow)
+    by_column = logit_grad.T.astype(narrow)
+    full[:, :hw] = dot(by_row, left) + dot(by_column, left)
+    full[:, hw:] = dot(by_row, right) + dot(by_column, right)
+    g = full[pl.ds(pl.multiple_of(device * 8, 8), 8), :] * 100.0
+    grad_o[...] = scale * g - p * (scale * scale * scale) * jnp.sum(p * g, -1, keepdims=True)
+    wires.finish()
+
+
+def run_contrast(bucket, pooled, devices):
+    rows, width = pooled.shape
+    slots = rows * devices
+    dma = pltpu.SemaphoreType.DMA
+    spec_v = pl.BlockSpec(memory_space=VM)
+    copies = 1 + 2 + 12 + 16
+    loss, grad = pl.pallas_call(
+        functools.partial(contrast_kernel, slots, bucket.shape[0]),
+        out_shape=[jax.ShapeDtypeStruct((8, 128), single), jax.ShapeDtypeStruct(pooled.shape, single)],
+        in_specs=[pl.BlockSpec(memory_space=SM), spec_v],
+        out_specs=[spec_v, spec_v],
+        scratch_shapes=[
+            VM((2 * rows, width // 2), narrow), VM((devices, 2 * rows, width // 2), narrow), VM((slots, width), single),
+            dma((copies,)), dma((copies,)), dma(()),
+        ],
+        compiler_params=pltpu.CompilerParams(collective_id=3, has_side_effects=True),
+        name="contrast",
+    )(bucket, pooled)
+    return loss[0, 0], grad
+
+
 def gather_weights(tab, w_in, w_out, w_up, w_down, small):
     gat = lambda a: lax.all_gather(a, "fsdp", axis=0, tiled=True)
     return lax.all_gather(tab, "fsdp", axis=1, tiled=True), gat(w_in), gat(w_out), gat(w_up), gat(w_down), gat(small)
@@ -687,8 +1157,8 @@
 
 def reduce_all(grads, small):
     done = []
-    for a, axis in grads:
-        part = lax.psum_scatter(a.astype(single), "fsdp", scatter_dimension=axis, tiled=True)
+    for a in grads:
+        part = lax.psum_scatter(a.astype(single), "fsdp", scatter_dimension=0, tiled=True)
         done.append(lax.psum(part.astype(narrow), "dp").astype(single))
     return done, lax.psum(small, ("dp", "fsdp"))
 
@@ -707,30 +1177,48 @@
     small_parts = (query_bias, value_bias, out_bias, first_gain, first_shift, down_bias, second_gain, second_shift)
     piece = query_bias.shape[0]
     wide_piece = up_bias.shape[0]
-    small = jnp.concatenate(small_parts + (up_bias,))[None, :]
-    table, w_in, w_out, w_up, w_down, small_all = gather_weights(
-        position_table, in_projection, out_projection, up_projection, down_projection, small
-    )
-    heads = small_all[:, : 8 * piece].reshape(shards, 8, piece).transpose(1, 0, 2).reshape(8, width)
-    vecs = jnp.concatenate(
-        [heads, small_all[:, 8 * piece :].reshape(ff // width, width), jnp.zeros((8 - ff // width, width), narrow)]
-    ).astype(single)
     flag = lax.dynamic_slice_in_dim(jnp.repeat(bucket, 2), device * groups, groups)
-    weights = (w_in, w_out, w_up, w_down)
+    chunks = ff // width
+    grid = lax.axis_size("dp") == 4 and shards == 8
+    if grid:
+        line = jnp.concatenate([v[None] for v in small_parts] + [jnp.zeros((8, piece), narrow)], 0)
+        spread = lax.dynamic_update_slice(jnp.zeros((16, width), narrow), line, (0, fs * piece))
+        ups = lax.dynamic_update_slice(jnp.zeros((ff,), narrow), up_bias, (fs * wide_piece,)).reshape(chunks, width)
+        spread = lax.dynamic_update_slice(spread, ups, (8, 0))
+        small_all, table_t, *weights = run_gather(
+            spread, (position_table.T, in_projection, out_projection, up_projection, down_projection)
+        )
+        vecs = jnp.sum(small_all.astype(single), 0)
+        table = table_t.T
+    else:
+        small = jnp.concatenate(small_parts + (up_bias,))[None, :]
+        table, *weights, small_all = gather_weights(
+            position_table, in_projection, out_projection, up_projection, down_projection, small
+        )
+        heads = small_all[:, : 8 * piece].reshape(shards, 8, piece).transpose(1, 0, 2).reshape(8, width)
+        vecs = jnp.concatenate(
+            [heads, small_all[:, 8 * piece :].reshape(chunks, width), jnp.zeros((8 - chunks, width), narrow)]
+        ).astype(single)
     *saved, pooled = run_forward(groups, count, width, ff, lengths, flag, vecs, tokens, table, weights)
-    embedded, norm_grad = jax.vjp(normalize_rows, pooled)
-    every = lax.all_gather(embedded.astype(narrow), ("dp", "fsdp"), axis=0, tiled=True)
     slots = groups * 4
-    loss, embed_grad = contrast(every, embedded, device * slots, slots, bucket)
-    pooled_grad = norm_grad(embed_grad)[0]
+    if grid:
+        loss, pooled_grad = run_contrast(bucket, pooled, 4 * shards)
+    else:
+        embedded, norm_grad = jax.vjp(normalize_rows, pooled)
+        every = lax.all_gather(embedded.astype(narrow), ("dp", "fsdp"), axis=0, tiled=True)
+        loss, embed_grad = contrast(every, embedded, device * slots, slots, bucket)
+        pooled_grad = norm_grad(embed_grad)[0]
     tokens_grad, gin, gout, gup, gdown, gtab, gvec = run_backward(
         groups, count, width, ff, lengths, flag, vecs, pooled_grad, weights, saved
     )
-    (gin, gout, gup, gdown, gtab), gvec = reduce_all(((gin, 0), (gout, 0), (gup, 0), (gdown, 1), (gtab, 0)), gvec)
-    gdown = gdown.T
+    if grid:
+        cut = lambda a: a.reshape(4, 2, a.shape[0] // 8, a.shape[1])
+        gdown, gup, gout, gin, gtab, gvec = run_reduce([cut(a) for a in (gdown, gup, gout, gin, gtab)], gvec)
+    else:
+        (gin, gout, gup, gdown, gtab), gvec = reduce_all((gin, gout, gup, gdown, gtab), gvec)
     gtab = gtab.T
     own = [lax.dynamic_slice_in_dim(gvec[i], fs * piece, piece) for i in range(8)]
-    up_own = lax.dynamic_slice_in_dim(gvec[8 : 8 + ff // width].reshape(ff), fs * wide_piece, wide_piece)
+    up_own = lax.dynamic_slice_in_dim(gvec[8 : 8 + chunks].reshape(ff), fs * wide_piece, wide_piece)
     return (
         loss, pooled, tokens_grad, gtab, gin, own[0], own[1], gout, own[2], own[3], own[4], gup, up_own, gdown,
         own[5], own[6], own[7],

time: 718 us -> 350 us (0.49)
  waiting for transfers between devices: 413 us -> 0 us
  Pallas kernels: 133 us -> 327 us
  blocking collectives: 113 us -> 0 us
  other arithmetic: 26.3 us -> 1.58 us
  between operations: 16.8 us -> 0.76 us
    reduce_scatter x5 -> x0, waiting for transfers between devices: 251 us -> none  [reduce_all(): lax.psum_scatter(a.astype(single), 'fsdp', scatter_dimension=axis, tiled=...]
    pallas_call x0 -> x3, Pallas kernels: none -> 194 us  [the longest x1 99.1 us: run_reduce(): pl.pallas_call(functools.partial(reduce_kernel, count), out_shape=[jax.Sh...]
    all_gather x4 -> x0, waiting for transfers between devices: 129 us -> none  [gather_weights(): gat = lambda a: lax.all_gather(a, 'fsdp', axis=0, tiled=True)]
    all_gather x3 -> x0, blocking collectives: 74.9 us -> none  [the longest x1 41.1 us: local(): lax.all_gather(embedded.astype(narrow), ('dp', 'fsdp'), axis=0, tiled=True)]
    psum x1 -> x0, blocking collectives: 38.6 us -> none  [reduce_all(): return (done, lax.psum(small, ('dp', 'fsdp')))]
    psum x1 -> x0, waiting for transfers between devices: 27.8 us -> none  [reduce_all(): done.append(lax.psum(part.astype(narrow), 'dp').astype(single))]
    convert_element_type x8 -> x0, other arithmetic: 17.2 us -> none  [the longest x2 9.76 us: reduce_all(): a.astype(single)]
  transfers between devices with their start and end apart: 10 -> 0, of which waited for: 9 -> 0; matrix products, arithmetic and copies ran while one was open for 4% -> 0% of each run, Pallas kernels for 0% -> 0%
where the time goes in v2:
time: 350 us; the launch traced here: 349 us
  Pallas kernels  327 us (93%)
  local copies, waits for them, and re-layouts  19.9 us (6%)
    pallas_call x1, Pallas kernels, run_reduce(): pl.pallas_call(functools.partial(reduce_kernel, count), out_shape=[jax.Sh...  99.1 us
    pallas_call x1, Pallas kernels, run_backward(): pl.pallas_call(functools.partial(backward_kernel, (groups, count, width,...  75.6 us
    pallas_call x1, Pallas kernels, run_gather(): pl.pallas_call(functools.partial(gather_kernel, count), out_shape=[jax.Sh...  73.3 us
    pallas_call x1, Pallas kernels, run_forward(): pl.pallas_call(functools.partial(forward_kernel, (groups, count, width, f...  57.4 us
    pallas_call x1, Pallas kernels, run_contrast(): pl.pallas_call(functools.partial(contrast_kernel, slots, bucket.shape[0])...  21.5 us
    unnamed x11, local copies, waits for them, and re-layouts  8.08 us

profile of v2, /device:TPU:0, one launch (start us, length us, event | category | flops | bytes accessed | tf_op | source)
XLA Modules:
  0.0 349.2 jit_solution(18245086798838761425)
XLA Ops:
  0.7 0.7 broadcast_in_dim.36
  1.4 0.1 reshape.66
  1.5 0.6 dynamic_slice.46.flag
  2.1 0.8 concatenate.3
  2.9 0.2 dynamic_update_slice.9
  3.1 0.9 dynamic_update_slice.10
  4.0 0.0 copy-start.2
  4.0 0.6 copy-done.2
  4.6 73.3 %gather_weights.1 = (bf16[8,16,768]{2,1,0:T(8,128)(2,1)}, bf16[768,512]{1,0:T(8,128)(2,1)}, bf16[768,2304]{1,0:T(8,128)(2,1)}, bf16[768,768]{1,0:T(8,128)(2,1)},...) custom-call(bf16[16,768]{1,0:T(8,128)(2,1)} %copy-done.2, bf16[96,512]{1,0:T(8,128)(2,1)} %bitcast.40, ...), custom_call_target="tpu_custom_call" | custom-call | tf_op jit(solution)/shard_map/gather_weights/pallas_call | solution.py:841
  77.9 1.6 convert_reduce_fusion.vecs
  79.5 2.3 copy.35
  81.8 57.4 %encoder_forward.1 = (bf16[1024,768]{1,0:T(8,128)(2,1)}, bf16[1024,2304]{1,0:T(8,128)(2,1)}, bf16[12,2,512,512]{3,2,1,0:T(8,128)(2,1)}, bf16[1024,768]{1,0:T(8,1...) custom-call(s32[2,4]{1,0:T(2,128)} %lens.3, ...), custom_call_target="tpu_custom_call" | custom-call | flops 14495514624 | bytes 83886080 | tf_op jit(solution)/shard_map/encoder_forward/pallas_call | solution.py:561
  139.2 21.5 %contrast.1 = (f32[8,128]{1,0:T(8,128)}, f32[8,768]{1,0:T(8,128)}) custom-call(s32[32]{0:T(128)} %bucket.1, f32[8,768]{1,0:T(8,128)} %get-tuple-element.115.pooled), custom_call_target="tpu_custom_call" | custom-call | tf_op jit(solution)/shard_map/contrast/pallas_call | solution.py:1138
  160.7 1.2 slice.30
  161.9 75.6 %encoder_backward.1 = (f32[1024,768]{1,0:T(8,128)}, bf16[768,2304]{1,0:T(8,128)(2,1)}, bf16[768,768]{1,0:T(8,128)(2,1)}, bf16[768,3072]{1,0:T(8,128)(2,1)}, bf16...) custom-call(s32[2,4]{1,0:T(2,128)} %lens.3, s32[2]{0:T(128)} %dynamic_slice.46.flag, ...), custom_call_target="tpu_custom_call" | custom-call | flops 28991029248 | bytes 104857600 | tf_op jit(solution)/shard_map/encoder_backward/pallas_call | solution.py:599
  237.6 99.1 %reduce_gradients.1 = (f32[384,768]{1,0:T(8,128)}, f32[96,3072]{1,0:T(8,128)}, f32[96,768]{1,0:T(8,128)}, f32[96,2304]{1,0:T(8,128)}, f32[96,512]{1,0:T(8,128)}, /*index=5*/f32[16,768]{1,0:T(8,128)}) custom-call(f32[16,768]{1,0:T(8,128)} %get-tuple-element.69.small, bf16[4,2,384,768]{3,2,1,0:T(8,128)(2,1)} %bitcast.34, bf16[4,2,96,3072]{3,2,1,0:T(8,128)(2,1)} %bitcast.33, ...), custom_call_target="tpu_custom_call" | custom-call | tf_op jit(solution)/shard_map/reduce_gradients/pallas_call | solution.py:1030
  336.7 0.0 copy-start.1
  336.7 0.0 copy-start
  336.7 1.2 fusion.8
  338.0 0.6 fusion
  338.6 0.6 fusion.2
  339.1 0.6 fusion.4
  339.7 0.7 slice.36
  340.5 0.7 dynamic_slice.57
  341.1 0.6 fusion.6
  341.7 1.6 copy.44
  343.3 2.1 copy.45
  345.5 1.7 copy.46
  347.2 0.0 copy-done.1
  347.2 1.0 copy.47
  348.2 0.0 copy-done
  348.2 1.0 copy.48
  (6 shorter events, 0.1 us)
Async XLA Ops:
  4.0 0.6 copy-start.2
  336.7 10.5 %copy-start.1 = (f32[96,3072]{1,0:T(8,128)S(1)}, f32[96,3072]{1,0:T(8,128)}, u32[]{:S(2)}) copy-start(f32[96,3072]{1,0:T(8,128)} %get-tuple-element.125) | copy-start | bytes 3538948
  336.7 11.5 %copy-start = (f32[384,768]{1,0:T(8,128)S(1)}, f32[384,768]{1,0:T(8,128)}, u32[]{:S(2)}) copy-start(f32[384,768]{1,0:T(8,128)} %get-tuple-element.127) | copy-start | bytes 3538948
